TPU v7x, 32 devices: a whole 2x2x4 slice. The times are simulated.
32 devices in a mesh: grp: 4 (over z), tok: 8 (over y, x, core).
Axes of the slice: x: 2, y: 2, z: 4, core: 2. Of those that a mesh axis runs over, the one named last changes fastest.
Arguments:
- tokens: bfloat16 [4, 2, 8192, 512], P('grp', None, 'tok'), may hold values from -6 to 6
- latents: float32 [4, 2, 2048, 512], P('grp'), may hold values from -6 to 6
- segments: int32 [4, 2, 8192], P('grp', None, 'tok'), may hold values from 0 to 7, as said below
- scene_mask: int32 [4, 2, 8, 8], P('grp'), may hold values from 0 to 1
- counts: int32 [4, 2, 8], P('grp', None, 'tok'), may hold values from 512 to 1024, as said below
- token_gain: float32 [512], replicated, may hold values from 0.1 to 1.9
- query_gain: float32 [512], replicated, may hold values from 0.1 to 1.9
- query_weight: bfloat16 [512, 512], replicated, may hold values from -0.5 to 0.5
- key_weight: bfloat16 [512, 512], replicated, may hold values from -0.25 to 0.25
- value_weight: bfloat16 [512, 512], replicated, may hold values from -0.25 to 0.25
- output_weight: bfloat16 [512, 512], replicated, may hold values from -4 to 4
- first_gain: float32 [512], replicated, may hold values from 0.1 to 1.9
- first_up: bfloat16 [512, 2048], replicated, may hold values from -0.25 to 0.25
- first_down: bfloat16 [2048, 512], replicated, may hold values from -0.25 to 0.25
- mixer_gain: float32 [512], replicated, may hold values from 0.1 to 1.9
- mixer_project: bfloat16 [512, 1536], replicated, may hold values from -0.25 to 0.25
- mixer_output: bfloat16 [512, 512], replicated, may hold values from -6 to 6
- second_gain: float32 [512], replicated, may hold values from 0.1 to 1.9
- second_up: bfloat16 [512, 2048], replicated, may hold values from -0.25 to 0.25
- second_down: bfloat16 [2048, 512], replicated, may hold values from -0.25 to 0.25
- cotangent: float32 [4, 2, 2048, 512], P('grp', None, 'tok'), may hold values from -6 to 6
Outputs:
- latents_out: float32 [4, 2, 2048, 512], P('grp', None, 'tok')
- latents_grad: float32 [4, 2, 2048, 512], P('grp', None, 'tok')
- tokens_grad: float32 [4, 2, 8192, 512], P('grp', None, 'tok')
- grad_token_gain: float32 [512], P('tok')
- grad_query_gain: float32 [512], P('tok')
- grad_query_weight: float32 [512, 512], P('tok')
- grad_key_weight: float32 [512, 512], P('tok')
- grad_value_weight: float32 [512, 512], P('tok')
- grad_output_weight: float32 [512, 512], P('tok')
- grad_first_gain: float32 [512], P('tok')
- grad_first_up: float32 [512, 2048], P('tok')
- grad_first_down: float32 [2048, 512], P('tok')
- grad_mixer_gain: float32 [512], P('tok')
- grad_mixer_project: float32 [512, 1536], P('tok')
- grad_mixer_output: float32 [512, 512], P('tok')
- grad_second_gain: float32 [512], P('tok')
- grad_second_up: float32 [512, 2048], P('tok')
- grad_second_down: float32 [2048, 512], P('tok')
Inputs may be any that keep to these rules, and one draw needn't show every extreme that they name: `segments`: scenes come in runs of 32 tokens; in every set one scene holds the first 32 tokens of every device's share, and every latent group sees it. The first counts tokens of a device's share of a set are live, the rest are padding that no latent sees; in every set some device is full.
All inputs are finite; a program needn't handle non-finite values.
Results may differ from a plain program's by a relative error of at most 0.034.
Values may be sent and summed in bfloat16 or wider, within the bound.
A program may use at most 256 MiB of HBM per device.

v0:
```python
import functools

import jax
import jax.numpy as jnp
from jax import lax
from jax.experimental import pallas as pl
from jax.experimental.pallas import tpu as pltpu
from jax.sharding import PartitionSpec as P

D = 512
L = 2048
H = 8
HD = 64
TOK_DEV = 1024
MB = 2
SCENES = 8
LGROUPS = 8


EPS = 1e-05
NEG = -1e30


def norm_rows(values, gain):
    centre = values - jnp.mean(values, axis=-1, keepdims=True)
    spread = jnp.mean(centre * centre, axis=-1, keepdims=True)
    return centre * lax.rsqrt(spread + EPS) * gain


def norm_back(values, gain, upstream):
    unused, pull = jax.vjp(norm_rows, values, gain)
    return pull(upstream)


def gelu_back(hidden, upstream):
    unused, pull = jax.vjp(jax.nn.gelu, hidden)
    return pull(upstream)[0]


def product_plain(left, right):
    return jnp.dot(left, right, preferred_element_type=jnp.float32)


def product_rows(left, right):
    return lax.dot_general(
        left, right, (((0,), (0,)), ((), ())), preferred_element_type=jnp.float32
    )


def product_cols(left, right):
    return lax.dot_general(
        left, right, (((1,), (1,)), ((), ())), preferred_element_type=jnp.float32
    )


def add_term(store, name, value):
    if name in store:
        store[name] = store[name] + value
    else:
        store[name] = value


def project_tokens(tokens, member, token_gain, key_weight, value_weight):
    source = tokens[0, member].astype(jnp.float32)
    normed = norm_rows(source, token_gain).astype(jnp.bfloat16)
    key_rows = product_plain(normed, key_weight).astype(jnp.bfloat16)
    value_rows = product_plain(normed, value_weight).astype(jnp.bfloat16)
    return (source, normed, key_rows, value_rows)


def mlp_forward(residual, gain, up_weight, down_weight):
    normed = norm_rows(residual, gain).astype(jnp.bfloat16)
    hidden = product_plain(normed, up_weight)
    active = jax.nn.gelu(hidden).astype(jnp.bfloat16)
    return (residual + product_plain(active, down_weight), (normed, hidden, active))


def mlp_backward(residual, gain, up_weight, down_weight, saved, upstream):
    normed, hidden, active = saved
    grad_low = upstream.astype(jnp.bfloat16)
    grad_down = product_rows(active, grad_low)
    hidden_grad = gelu_back(hidden, product_cols(grad_low, down_weight)).astype(jnp.bfloat16)
    grad_up = product_rows(normed, hidden_grad)
    residual_grad, grad_gain = norm_back(residual, gain, product_cols(hidden_grad, up_weight))
    return (upstream + residual_grad, grad_gain, grad_up, grad_down)


def mixer_forward(residual, gain, project, output):
    own_rows = residual.shape[0]
    normed = norm_rows(residual, gain).astype(jnp.bfloat16)
    packed = product_plain(normed, project).astype(jnp.bfloat16)
    pair_rows = lax.all_gather(packed[:, D:], "tok", axis=0, tiled=True)
    every = pair_rows.shape[0]
    own_queries = packed[:, :D].reshape(own_rows, H, HD)
    keys = pair_rows[:, :D].reshape(every, H, HD)
    values = pair_rows[:, D:].reshape(every, H, HD)
    logits = jnp.einsum(
        "qhd,khd->hqk", own_queries, keys, preferred_element_type=jnp.float32
    ) * HD ** (-0.5)
    peak_row = jnp.max(logits, axis=-1, keepdims=True)
    raised = jnp.exp(logits - peak_row)
    softened = raised / jnp.sum(raised, axis=-1, keepdims=True)
    softened_low = softened.astype(jnp.bfloat16)
    mixed_rows = jnp.einsum(
        "hqk,khd->qhd", softened_low, values, preferred_element_type=jnp.float32
    )
    mixed_rows = mixed_rows.reshape(own_rows, D).astype(jnp.bfloat16)
    return (
        residual + product_plain(mixed_rows, output),
        (normed, own_queries, keys, values, softened, softened_low, mixed_rows),
    )


def mixer_backward(residual, gain, project, output, saved, upstream):
    normed, own_queries, keys, values, softened, softened_low, mixed_rows = saved
    own_rows = upstream.shape[0]
    every = keys.shape[0]
    grad_low = upstream.astype(jnp.bfloat16)
    grad_output = product_rows(mixed_rows, grad_low)
    mixed_grad = product_cols(grad_low, output).astype(jnp.bfloat16).reshape(own_rows, H, HD)
    value_grad = jnp.einsum(
        "hqk,qhd->khd", softened_low, mixed_grad, preferred_element_type=jnp.float32
    )
    soft_grad = jnp.einsum("qhd,khd->hqk", mixed_grad, values, preferred_element_type=jnp.float32)
    logit_grad = softened * (soft_grad - jnp.sum(soft_grad * softened, axis=-1, keepdims=True))
    logit_grad = logit_grad.astype(jnp.bfloat16)
    query_grad = jnp.einsum(
        "hqk,khd->qhd", logit_grad, keys, preferred_element_type=jnp.float32
    ) * HD ** (-0.5)
    key_grad = jnp.einsum(
        "hqk,qhd->khd", logit_grad, own_queries, preferred_element_type=jnp.float32
    ) * HD ** (-0.5)
    pair_terms = jnp.concatenate([key_grad.reshape(every, D), value_grad.reshape(every, D)], axis=1)
    pair_grad = lax.psum_scatter(
        pair_terms.astype(jnp.bfloat16), "tok", scatter_dimension=0, tiled=True
    ).astype(jnp.float32)
    packed_grad = jnp.concatenate([query_grad.reshape(own_rows, D), pair_grad], axis=1).astype(
        jnp.bfloat16
    )
    grad_project = product_rows(normed, packed_grad)
    residual_grad, grad_gain = norm_back(residual, gain, product_cols(packed_grad, project))
    return (upstream + residual_grad, grad_gain, grad_project, grad_output)


def general_body(
    tokens,
    latents,
    segments,
    scene_mask,
    counts,
    token_gain,
    query_gain,
    query_weight,
    key_weight,
    value_weight,
    output_weight,
    first_gain,
    first_up,
    first_down,
    mixer_gain,
    mixer_project,
    mixer_output,
    second_gain,
    second_up,
    second_down,
    cotangent,
):
    scale = D ** (-0.5)
    shards = lax.axis_size("tok")
    own_rows = L // shards
    row_start = lax.axis_index("tok") * own_rows
    latent_group = jnp.arange(L) // (L // LGROUPS)
    latent_onehot = (latent_group[:, None] == jnp.arange(LGROUPS)[None, :]).astype(jnp.float32)
    token_place = jnp.arange(TOK_DEV)
    records = []
    latent_outs = []
    for member in range(MB):
        record = {}
        source, normed, key_rows, value_rows = project_tokens(
            tokens, member, token_gain, key_weight, value_weight
        )
        record["token_side"] = (source, normed, key_rows, value_rows)
        scene_onehot = (segments[0, member][:, None] == jnp.arange(SCENES)[None, :]).astype(
            jnp.float32
        )
        token_seen = jnp.dot(scene_onehot, scene_mask[0, member].astype(jnp.float32))
        visible = product_cols(latent_onehot, token_seen)
        alive = token_place < counts[0, member, 0]
        allowed = (visible > 0.5) & alive[None, :]
        latent_every = latents[0, member]
        normed_every = norm_rows(latent_every, query_gain).astype(jnp.bfloat16)
        queries = product_plain(normed_every, query_weight).astype(jnp.bfloat16)
        scores = jnp.where(allowed, product_cols(queries, key_rows) * scale, NEG)
        row_top = lax.pmax(jnp.max(scores, axis=1), "tok")
        unnormed = jnp.exp(scores - row_top[:, None])
        row_total, weighted = (
            lax.psum_scatter(
                jnp.sum(unnormed, axis=1).astype(jnp.bfloat16),
                "tok",
                scatter_dimension=0,
                tiled=True,
            ).astype(jnp.float32),
            lax.psum_scatter(
                product_plain(unnormed.astype(jnp.bfloat16), value_rows).astype(jnp.bfloat16),
                "tok",
                scatter_dimension=0,
                tiled=True,
            ).astype(jnp.float32),
        )
        latent_in = lax.dynamic_slice_in_dim(latent_every, row_start, own_rows, 0)
        latent_normed = lax.dynamic_slice_in_dim(normed_every, row_start, own_rows, 0)
        attended = weighted / row_total[:, None]
        attended_low = attended.astype(jnp.bfloat16)
        first_mid = latent_in + product_plain(attended_low, output_weight)
        mixer_mid, first_saved = mlp_forward(first_mid, first_gain, first_up, first_down)
        second_mid, mixer_saved = mixer_forward(mixer_mid, mixer_gain, mixer_project, mixer_output)
        final_rows, second_saved = mlp_forward(second_mid, second_gain, second_up, second_down)
        latent_outs.append(final_rows)
        record["latent_side"] = (
            allowed,
            latent_in,
            latent_normed,
            queries,
            row_top,
            row_total,
            attended,
            attended_low,
            first_mid,
            mixer_mid,
            second_mid,
            first_saved,
            mixer_saved,
            second_saved,
        )
        records.append(record)
    grads = {}
    latent_grads = []
    token_grads = []
    for member in range(MB):
        record = records[member]
        source, normed, key_rows, value_rows = record["token_side"]
        (
            allowed,
            latent_in,
            latent_normed,
            queries,
            row_top,
            row_total,
            attended,
            attended_low,
            first_mid,
            mixer_mid,
            second_mid,
            first_saved,
            mixer_saved,
            second_saved,
        ) = record["latent_side"]
        second_back = mlp_backward(
            second_mid, second_gain, second_up, second_down, second_saved, cotangent[0, member]
        )
        add_term(grads, "second_gain", second_back[1])
        add_term(grads, "second_up", second_back[2])
        add_term(grads, "second_down", second_back[3])
        mixer_back = mixer_backward(
            mixer_mid, mixer_gain, mixer_project, mixer_output, mixer_saved, second_back[0]
        )
        add_term(grads, "mixer_gain", mixer_back[1])
        add_term(grads, "mixer_project", mixer_back[2])
        add_term(grads, "mixer_output", mixer_back[3])
        first_back = mlp_backward(
            first_mid, first_gain, first_up, first_down, first_saved, mixer_back[0]
        )
        add_term(grads, "first_gain", first_back[1])
        add_term(grads, "first_up", first_back[2])
        add_term(grads, "first_down", first_back[3])
        latent_upstream = first_back[0]
        grad_low = latent_upstream.astype(jnp.bfloat16)
        add_term(grads, "output_weight", product_rows(attended_low, grad_low))
        attended_grad = lax.optimization_barrier(
            product_cols(grad_low, output_weight).astype(jnp.bfloat16)
        ).astype(jnp.float32)
        weighted_grad = (attended_grad / row_total[:, None]).astype(jnp.bfloat16)
        total_grad = -jnp.sum(attended_grad * attended, axis=1) / row_total
        weighted_every, total_every = (
            lax.all_gather(
                weighted_grad.astype(jnp.float32).astype(jnp.bfloat16), "tok", axis=0, tiled=True
            ).astype(jnp.float32),
            lax.all_gather(total_grad.astype(jnp.bfloat16), "tok", axis=0, tiled=True).astype(
                total_grad.dtype
            ),
        )
        weighted_every = weighted_every.astype(jnp.bfloat16)
        scores = jnp.where(allowed, product_cols(queries, key_rows) * scale, NEG)
        unnormed = jnp.exp(scores - row_top[:, None])
        unnormed_grad = product_cols(weighted_every, value_rows) + total_every[:, None]
        score_grad = (unnormed * unnormed_grad).astype(jnp.bfloat16)
        value_grad = product_rows(unnormed.astype(jnp.bfloat16), weighted_every).astype(
            jnp.bfloat16
        )
        key_grad = (product_rows(score_grad, queries) * scale).astype(jnp.bfloat16)
        query_grad = lax.psum_scatter(
            (product_plain(score_grad, key_rows) * scale).astype(jnp.bfloat16),
            "tok",
            scatter_dimension=0,
            tiled=True,
        )
        add_term(grads, "key_weight", product_rows(normed, key_grad))
        add_term(grads, "value_weight", product_rows(normed, value_grad))
        normed_grad = product_cols(key_grad, key_weight) + product_cols(value_grad, value_weight)
        source_grad, gain_grad = norm_back(source, token_gain, normed_grad)
        add_term(grads, "token_gain", gain_grad)
        token_grads.append(source_grad)
        add_term(grads, "query_weight", product_rows(latent_normed, query_grad))
        latent_grad, gain_grad = norm_back(
            latent_in, query_gain, product_cols(query_grad, query_weight)
        )
        add_term(grads, "query_gain", gain_grad)
        latent_grads.append(latent_upstream + latent_grad)
    parts = (
        lax.psum_scatter(
            grads["token_gain"].astype(jnp.bfloat16), "tok", scatter_dimension=0, tiled=True
        ).astype(jnp.float32),
        lax.psum_scatter(
            grads["query_gain"].astype(jnp.bfloat16), "tok", scatter_dimension=0, tiled=True
        ).astype(jnp.float32),
        lax.psum_scatter(
            grads["query_weight"].astype(jnp.bfloat16), "tok", scatter_dimension=0, tiled=True
        ).astype(jnp.float32),
        lax.psum_scatter(
            grads["key_weight"].astype(jnp.bfloat16), "tok", scatter_dimension=0, tiled=True
        ).astype(jnp.float32),
        lax.psum_scatter(
            grads["value_weight"].astype(jnp.bfloat16), "tok", scatter_dimension=0, tiled=True
        ).astype(jnp.float32),
        lax.psum_scatter(
            grads["output_weight"].astype(jnp.bfloat16), "tok", scatter_dimension=0, tiled=True
        ).astype(jnp.float32),
        lax.psum_scatter(
            grads["first_gain"].astype(jnp.bfloat16), "tok", scatter_dimension=0, tiled=True
        ).astype(jnp.float32),
        lax.psum_scatter(
            grads["first_up"].astype(jnp.bfloat16), "tok", scatter_dimension=0, tiled=True
        ).astype(jnp.float32),
        lax.psum_scatter(
            grads["first_down"].astype(jnp.bfloat16), "tok", scatter_dimension=0, tiled=True
        ).astype(jnp.float32),
        lax.psum_scatter(
            grads["mixer_gain"].astype(jnp.bfloat16), "tok", scatter_dimension=0, tiled=True
        ).astype(jnp.float32),
        lax.psum_scatter(
            grads["mixer_project"].astype(jnp.bfloat16), "tok", scatter_dimension=0, tiled=True
        ).astype(jnp.float32),
        lax.psum_scatter(
            grads["mixer_output"].astype(jnp.bfloat16), "tok", scatter_dimension=0, tiled=True
        ).astype(jnp.float32),
        lax.psum_scatter(
            grads["second_gain"].astype(jnp.bfloat16), "tok", scatter_dimension=0, tiled=True
        ).astype(jnp.float32),
        lax.psum_scatter(
            grads["second_up"].astype(jnp.bfloat16), "tok", scatter_dimension=0, tiled=True
        ).astype(jnp.float32),
        lax.psum_scatter(
            grads["second_down"].astype(jnp.bfloat16), "tok", scatter_dimension=0, tiled=True
        ).astype(jnp.float32),
    )
    summed = (
        lax.psum(parts[0].astype(jnp.bfloat16), "grp").astype(jnp.float32),
        lax.psum(parts[1].astype(jnp.bfloat16), "grp").astype(jnp.float32),
        lax.psum(parts[2].astype(jnp.bfloat16), "grp").astype(jnp.float32),
        lax.psum(parts[3].astype(jnp.bfloat16), "grp").astype(jnp.float32),
        lax.psum(parts[4].astype(jnp.bfloat16), "grp").astype(jnp.float32),
        lax.psum(parts[5].astype(jnp.bfloat16), "grp").astype(jnp.float32),
        lax.psum(parts[6].astype(jnp.bfloat16), "grp").astype(jnp.float32),
        lax.psum(parts[7].astype(jnp.bfloat16), "grp").astype(jnp.float32),
        lax.psum(parts[8].astype(jnp.bfloat16), "grp").astype(jnp.float32),
        lax.psum(parts[9].astype(jnp.bfloat16), "grp").astype(jnp.float32),
        lax.psum(parts[10].astype(jnp.bfloat16), "grp").astype(jnp.float32),
        lax.psum(parts[11].astype(jnp.bfloat16), "grp").astype(jnp.float32),
        lax.psum(parts[12].astype(jnp.bfloat16), "grp").astype(jnp.float32),
        lax.psum(parts[13].astype(jnp.bfloat16), "grp").astype(jnp.float32),
        lax.psum(parts[14].astype(jnp.bfloat16), "grp").astype(jnp.float32),
    )
    return (
        jnp.stack(latent_outs)[None],
        jnp.stack(latent_grads)[None],
        jnp.stack(token_grads)[None],
    ) + tuple(summed)


TOK = 8
ROWS = L // TOK
FF = 2048
GR = L // LGROUPS
LOG2E = 1.4426950408889634
LN2 = 0.6931471805599453
F32 = jnp.float32
BF16 = jnp.bfloat16
MIB = 1024 * 1024


def nn(left, right):
    return lax.dot_general(left, right, (((1,), (0,)), ((), ())), preferred_element_type=F32)


def nt(left, right):
    return lax.dot_general(left, right, (((1,), (1,)), ((), ())), preferred_element_type=F32)


def tn(left, right):
    return lax.dot_general(left, right, (((0,), (0,)), ((), ())), preferred_element_type=F32)


def norm_parts(values):
    centre = values - jnp.mean(values, axis=-1, keepdims=True)
    inverse = lax.rsqrt(jnp.mean(centre * centre, axis=-1, keepdims=True) + EPS)
    return centre * inverse, inverse


def norm_pull(hat, inverse, gain, upstream):
    scaled = upstream * gain
    inner = jnp.mean(scaled * hat, axis=-1, keepdims=True)
    grad = (scaled - jnp.mean(scaled, axis=-1, keepdims=True) - hat * inner) * inverse
    return grad, upstream * hat


def places():
    me = lax.axis_index("tok")
    core = lax.rem(me, 2)
    chip = lax.div(me, 2)
    mate = me + 1 - 2 * core
    flip_x = chip + 1 - 2 * lax.rem(chip, 2)
    flip_y = lax.rem(chip + 2, 4)
    far = 3 - chip
    return me, core, chip, mate, (far, flip_x, flip_y)


def remote(src, dst, send_sem, recv_sem, peer):
    return pltpu.make_async_remote_copy(
        src_ref=src,
        dst_ref=dst,
        send_sem=send_sem,
        recv_sem=recv_sem,
        device_id={"tok": peer},
        device_id_type=pl.DeviceIdType.MESH,
    )


def greet(devices):
    barrier = pltpu.get_barrier_semaphore()
    for device in devices:
        pl.semaphore_signal(
            barrier, inc=1, device_id={"tok": device}, device_id_type=pl.DeviceIdType.MESH
        )
    pl.semaphore_wait(barrier, len(devices))


def chip_at(chip, flip):
    high, low = divmod(flip, 2) if isinstance(flip, int) else (lax.div(flip, 2), lax.rem(flip, 2))
    across = lax.rem(lax.rem(chip, 2) + low, 2)
    along = lax.rem(lax.div(chip, 2) + high, 2)
    return 2 * along + across


def mask_loads(seg_ref, mask_ref, seg_buf, mask_buf, sem):
    return (
        pltpu.make_async_copy(seg_ref.at[0], seg_buf, sem.at[0]),
        pltpu.make_async_copy(mask_ref.at[0], mask_buf, sem.at[1]),
    )


def mask_rows(seg_buf, mask_buf, count_ref, bias_ref):
    for member in range(MB):
        scene = lax.broadcasted_iota(jnp.int32, (SCENES, TOK_DEV), 0)
        place = lax.broadcasted_iota(jnp.int32, (SCENES, TOK_DEV), 1)
        hot = jnp.where((seg_buf[member:member + 1] == scene) & (place < count_ref[0, member, 0]), 1.0, 0.0)
        seen = tn(jnp.where(mask_buf[member] > 0, 1.0, 0.0).astype(BF16), hot.astype(BF16))
        bias_ref[member] = jnp.where(seen > 0.5, 0.0, NEG)


def to_rows(first, second):
    rows = first.shape[0]
    lane = lax.broadcasted_iota(jnp.int32, (rows, 128), 1)
    return jnp.where(lane == 0, first, second).T[0:8]


def cross_forward_kernel(
    tok_ref, lat_ref, tgain_ref, qgain_ref, qw_ref, kw_ref, vw_ref, seg_ref, mask_ref, count_ref,
    k_out, v_out, q_out, att_ref, lse_ref,
    tok_buf, lat_buf, keys, values, queries, bias, part, part_s, got, got_s, stage, stage_s,
    arrive, arrive_s, total, seg_buf, mask_buf,
    mask_sem, tok_sem, lat_sem, k_sem, v_sem, q_sem,
    core_send, core_recv, core_send_s, core_recv_s, chip_send, chip_recv, chip_send_s, chip_recv_s,
):
    me, core, chip, mate, others = places()
    span = 2 * ROWS

    def unpack(step):
        return lax.div(step, 4), 3 - lax.rem(step, 4)

    def lat_copy(step):
        member, flip = unpack(step)
        start = pl.multiple_of(chip_at(chip, flip) * span, span)
        return pltpu.make_async_copy(lat_ref.at[0, member, pl.ds(start, span)], lat_buf.at[step], lat_sem.at[step])

    def q_copy(step):
        member, flip = unpack(step)
        start = pl.multiple_of(chip_at(chip, flip) * span, span)
        return pltpu.make_async_copy(queries.at[step], q_out.at[member, pl.ds(start, span)], q_sem.at[step])

    def tok_copy(member):
        return pltpu.make_async_copy(tok_ref.at[0, member], tok_buf.at[member], tok_sem.at[member])

    def kv_copies(member):
        return (
            pltpu.make_async_copy(keys.at[member], k_out.at[member], k_sem.at[member]),
            pltpu.make_async_copy(values.at[member], v_out.at[member], v_sem.at[member]),
        )

    def core_copies(step):
        return (
            remote(part.at[step, 1 - core], got.at[step], core_send.at[step], core_recv.at[step], mate),
            remote(part_s.at[step, 1 - core], got_s.at[step], core_send_s.at[step], core_recv_s.at[step], mate),
        )

    def chip_copies(step):
        member, flip = unpack(step)
        peer = 2 * chip_at(chip, flip) + core
        place = 3 * member + flip - 1
        return (
            remote(stage.at[step], arrive.at[place], chip_send.at[place], chip_recv.at[place], peer),
            remote(stage_s.at[step], arrive_s.at[place], chip_send_s.at[place], chip_recv_s.at[place], peer),
        )

    tok_copy(0).start()
    masks = mask_loads(seg_ref, mask_ref, seg_buf, mask_buf, mask_sem)
    for copy in masks:
        copy.start()
    for step in range(4):
        lat_copy(step).start()
    tok_copy(1).start()
    for step in range(4, 2 * 4):
        lat_copy(step).start()
    greet([mate] + [2 * other + core for other in others])
    for copy in masks:
        copy.wait()
    mask_rows(seg_buf, mask_buf, count_ref, bias)

    def project(member):
        tok_copy(member).wait()
        hat, inverse = norm_parts(tok_buf[member].astype(F32))
        normed = (hat * tgain_ref[...]).astype(BF16)
        keys[member] = nn(normed, kw_ref[...]).astype(BF16)
        values[member] = nn(normed, vw_ref[...]).astype(BF16)
        for copy in kv_copies(member):
            copy.start()

    def ask(step):
        hat, inverse = norm_parts(lat_buf[step])
        normed = (hat * qgain_ref[...]).astype(BF16)
        queries[step] = (nn(normed, qw_ref[...]) * (D ** (-0.5) * LOG2E)).astype(BF16)

    def compute(step, ahead):
        member, flip = unpack(step)

        @pl.when(flip == 3)
        def _():
            project(member)

        if ahead:
            lat_copy(step + 1).wait()
        scores = nt(queries[step], keys[member])
        if ahead:
            ask(step + 1)
        raised = []
        for half in range(2):
            seen = bias[member, pl.ds(2 * chip_at(chip, flip) + half, 1), :]
            own = scores[half * ROWS:(half + 1) * ROWS] + seen
            top = jnp.max(own, axis=1, keepdims=True)
            own = jnp.exp2(own - top)
            part_s[step, half] = to_rows(top, jnp.sum(own, axis=1, keepdims=True))
            raised.append(own.astype(BF16))
        sums = nn(jnp.concatenate(raised, axis=0), values[member]).astype(BF16)
        for half in range(2):
            part[step, half] = sums[half * ROWS:(half + 1) * ROWS]
        for copy in core_copies(step):
            copy.start()
        if ahead:
            q_copy(step + 1).start()

    def merge(one, one_s, two, two_s):
        top = jnp.maximum(one_s[0:1], two_s[0:1])
        one_w, two_w = jnp.exp2(one_s[0:1] - top), jnp.exp2(two_s[0:1] - top)
        sums = one_s[1:2] * one_w + two_s[1:2] * two_w
        spare = jnp.zeros((6, ROWS), F32)
        weights = jnp.concatenate([one_w, two_w, spare], axis=0).T
        return one * weights[:, 0:1] + two * weights[:, 1:2], jnp.concatenate([top, sums, spare], axis=0)

    def combine(step):
        member, flip = unpack(step)
        for copy in core_copies(step):
            copy.wait_recv()
        added, figures = merge(
            part[step, core].astype(F32), part_s[step, core], got[step].astype(F32), got_s[step]
        )
        stage_s[step] = figures

        @pl.when(flip > 0)
        def _():
            stage[step] = added.astype(BF16)
            for copy in chip_copies(step):
                copy.start()

        @pl.when(flip == 0)
        def _():
            total[member] = added

    def finish(member):
        added, figures = total[member], stage_s[4 * member + 3]
        for flip in (1, 2, 3):
            for copy in chip_copies(4 * member + 3 - flip):
                copy.wait_recv()
            place = 3 * member + flip - 1
            added, figures = merge(added, figures, arrive[place].astype(F32), arrive_s[place])
        spare = jnp.zeros((7, ROWS), F32)
        inverse = jnp.concatenate([1.0 / figures[1:2], spare], axis=0).T
        att_ref[member] = added * inverse[:, 0:1]
        lse_ref[member] = jnp.concatenate([figures[0:1] + jnp.log2(figures[1:2]), spare], axis=0)

    def step_body(step, carry):
        compute(step, True)

        @pl.when(step > 0)
        def _():
            combine(step - 1)

        return carry

    last = jnp.int32(4 * MB - 1)
    lat_copy(jnp.int32(0)).wait()
    ask(0)
    q_copy(jnp.int32(0)).start()
    lax.fori_loop(0, 4 * MB - 1, step_body, 0)
    compute(last, False)
    combine(last - 1)
    combine(last)
    for member in range(MB):
        finish(member)
    for member in range(MB):
        for copy in kv_copies(member):
            copy.wait()
        for slot in range(4):
            step = 4 * member + slot
            q_copy(step).wait()
            for copy in core_copies(step):
                copy.wait_send()
            if slot < 3:
                for copy in chip_copies(step):
                    copy.wait_send()


def cross_forward(collective_id, *args):
    dma = pltpu.SemaphoreType.DMA
    span = 2 * ROWS
    steps = 4 * MB
    vmem = pl.BlockSpec(memory_space=pltpu.VMEM)
    hbm = pl.BlockSpec(memory_space=pl.ANY)
    return pl.pallas_call(
        cross_forward_kernel,
        in_specs=[hbm, hbm] + [vmem] * 5 + [hbm, hbm, pl.BlockSpec(memory_space=pltpu.SMEM)],
        out_specs=[hbm, hbm, hbm, vmem, vmem],
        out_shape=[
            jax.ShapeDtypeStruct((MB, TOK_DEV, D), BF16),
            jax.ShapeDtypeStruct((MB, TOK_DEV, D), BF16),
            jax.ShapeDtypeStruct((MB, L, D), BF16),
            jax.ShapeDtypeStruct((MB, ROWS, D), F32),
            jax.ShapeDtypeStruct((MB, 8, ROWS), F32),
        ],
        scratch_shapes=[
            pltpu.VMEM((MB, TOK_DEV, D), BF16),
            pltpu.VMEM((steps, span, D), F32),
            pltpu.VMEM((MB, TOK_DEV, D), BF16),
            pltpu.VMEM((MB, TOK_DEV, D), BF16),
            pltpu.VMEM((steps, span, D), BF16),
            pltpu.VMEM((MB, LGROUPS, TOK_DEV), F32),
            pltpu.VMEM((steps, 2, ROWS, D), BF16),
            pltpu.VMEM((steps, 2, 8, ROWS), F32),
            pltpu.VMEM((steps, ROWS, D), BF16),
            pltpu.VMEM((steps, 8, ROWS), F32),
            pltpu.VMEM((steps, ROWS, D), BF16),
            pltpu.VMEM((steps, 8, ROWS), F32),
            pltpu.VMEM((3 * MB, ROWS, D), BF16),
            pltpu.VMEM((3 * MB, 8, ROWS), F32),
            pltpu.VMEM((MB, ROWS, D), F32),
            pltpu.VMEM((MB, TOK_DEV), jnp.int32),
            pltpu.VMEM((MB, SCENES, LGROUPS), jnp.int32),
            dma((2,)), dma((MB,)), dma((steps,)), dma((MB,)), dma((MB,)), dma((steps,)),
        ] + [dma((steps,))] * 4 + [dma((3 * MB,))] * 4,
        compiler_params=pltpu.CompilerParams(
            collective_id=collective_id, has_side_effects=True, vmem_limit_bytes=56 * MIB
        ),
        cost_estimate=pl.CostEstimate(
            flops=14 * 10**9, bytes_accessed=22 * 10**6, transcendentals=4 * 10**6
        ),
        name="cross_forward",
    )(*args)


def cross_backward_kernel(
    items, grad_items,
    tok_ref, tgain_ref, kw_ref, vw_ref, seg_ref, mask_ref, count_ref, k_ref, v_ref, q_ref, up_ref, fig_ref,
    lat_ref, lup_ref, qgain_ref, qw_ref, fgain_ref, mgain_ref, sgain_ref, *refs,
):
    count, more = len(items), len(grad_items)
    parts, sources = refs[:count], refs[count:count + more]
    refs = refs[count + more:]
    dlat_ref, dtok_ref, dkw_ref, dvw_ref, dqw_ref, gains_ref = refs[:6]
    sums, helds = refs[6:6 + count], refs[6 + count:6 + count + more]
    rest = refs[6 + count + more:]
    cut = CROSS_SCRATCH + 3 * count + 2
    grp, grp_devices = grp_steps(items, parts, (), rest[CROSS_SCRATCH:cut], sums)
    tok, near_devices = tok_steps(grad_items, sources, rest[cut:])
    (tok_buf, keys, values, queries, ups, figs, bias, part, got, stage, arrive, far_in, total, dk, dv, dkw, dvw,
     dgain_ref, lat, lup, seg_buf, mask_buf, mask_sem, tail_sem,
     tok_sem, k_sem, v_sem, q_sem, out_sem, near_send, near_recv, far_send, far_recv, on_send, on_recv, own_sem,
     fig_send, fig_recv, core_send, core_recv, chip_send, chip_recv, half_send, half_recv) = rest[:CROSS_SCRATCH]
    me, core, chip, mate, others = places()
    span = 2 * ROWS

    def slot_of(step):
        late = lax.div(step + 3, 8)
        member = jnp.where(step == 1, 1, late)
        flip = jnp.where(step < 2, 0, jnp.where(late == 0, step - 1, 8 - step))
        return member, flip

    def loads(step):
        member, flip = slot_of(step)
        start = pl.multiple_of(chip_at(chip, flip) * span, span)
        ring = lax.rem(step, 4)
        return pltpu.make_async_copy(q_ref.at[member, pl.ds(start, span)], queries.at[ring], q_sem.at[ring])

    def tok_copies(member):
        return (
            pltpu.make_async_copy(k_ref.at[member], keys.at[member], k_sem.at[member]),
            pltpu.make_async_copy(v_ref.at[member], values.at[member], v_sem.at[member]),
            pltpu.make_async_copy(tok_ref.at[0, member], tok_buf.at[member], tok_sem.at[member]),
        )

    def out_copy(member):
        return pltpu.make_async_copy(dk.at[member], dtok_ref.at[0, member], out_sem.at[member])

    def own_copies(member):
        slot = 4 * member
        return (
            pltpu.make_async_copy(up_ref.at[member], ups.at[slot, core], own_sem.at[member, 0]),
            pltpu.make_async_copy(fig_ref.at[member], figs.at[slot, core], own_sem.at[member, 1]),
        )

    def near_copies(member):
        slot = 4 * member
        return [
            remote(up_ref.at[member], ups.at[slot, core], near_send.at[member, 0], near_recv.at[member, 0], mate),
            remote(fig_ref.at[member], figs.at[slot, core], near_send.at[member, 1], near_recv.at[member, 1], mate),
        ]

    half_rows = (pl.ds(0, ROWS // 2), pl.ds(ROWS // 2, ROWS // 2))

    def far_copies(slot):
        member, flip = slot // 4, slot % 4
        peer = 2 * chip_at(chip, flip) + core
        if flip < 3:
            return [
                remote(up_ref.at[member], ups.at[slot, core], far_send.at[slot, 0], far_recv.at[slot, 0], peer),
                remote(fig_ref.at[member], figs.at[slot, core], far_send.at[slot, 1], far_recv.at[slot, 1], peer),
            ]
        copies = []
        for half, (held, toward) in enumerate(((1, 2), (2, 1))):
            copies.append(remote(
                ups.at[4 * member + held, core, half_rows[half]], ups.at[slot, core, half_rows[half]],
                far_send.at[slot, half], far_recv.at[slot, half], 2 * chip_at(chip, toward) + core,
            ))
        copies.append(remote(
            figs.at[4 * member + 1, core], figs.at[slot, core], fig_send.at[member], fig_recv.at[member],
            2 * chip_at(chip, 2) + core,
        ))
        return copies

    def on_copies(slot):
        return (
            remote(ups.at[slot, core], ups.at[slot, core], on_send.at[slot, 0], on_recv.at[slot, 0], mate),
            remote(figs.at[slot, core], figs.at[slot, core], on_send.at[slot, 1], on_recv.at[slot, 1], mate),
        )

    def pass_on(slot):
        for copy in far_copies(slot):
            copy.wait_recv()
        for copy in on_copies(slot):
            copy.start()

    def pass_near(member):
        pass_on(4 * member + 1)
        pass_on(4 * member + 2)
        for copy in far_copies(4 * member + 3):
            copy.start()

    def half_copy(member, half):
        return remote(
            stage.at[4 * member + 3, half_rows[half]], far_in.at[member, half], half_send.at[member, half],
            half_recv.at[member, half], 2 * chip_at(chip, half + 1) + core,
        )

    def half_copies(member):
        return [half_copy(member, half) for half in range(2)]

    def core_copy(step):
        member, flip = slot_of(step)
        slot, ring = 4 * member + flip, lax.rem(step, 4)
        return remote(part.at[ring, 1 - core], got.at[slot], core_send.at[slot], core_recv.at[slot], mate)

    def chip_copy(slot):
        member, flip = slot // 4, slot % 4
        peer = 2 * chip_at(chip, flip) + core
        place = 2 * member + flip - 1
        return remote(stage.at[slot], arrive.at[place], chip_send.at[place], chip_recv.at[place], peer)

    def relay(member):
        for half in range(2):
            half_copy(member, half).wait_recv()
            slot = 4 * member + 2 - half
            joined = stage.at[slot, half_rows[half]]
            add(joined, joined, far_in.at[member, half])
            chip_copy(slot).start()

    masks = mask_loads(seg_ref, mask_ref, seg_buf, mask_buf, mask_sem)
    for copy in masks:
        copy.start()
    own_rows = pl.ds(pl.multiple_of(me * ROWS, ROWS), ROWS)
    tails = (
        pltpu.make_async_copy(lat_ref.at[0, :, own_rows], lat, tail_sem.at[0]),
        pltpu.make_async_copy(lup_ref, lup, tail_sem.at[1]),
    )
    for copy in own_copies(0):
        copy.start()
    for copy in tok_copies(0):
        copy.start()
    for step in range(3):
        loads(jnp.int32(step)).start()
    for copy in own_copies(1):
        copy.start()
    for copy in tok_copies(1):
        copy.start()
    for copy in tails:
        copy.start()
    greet_all([mate] + [2 * other + core for other in others], grp_devices)
    for member in range(MB):
        for copy in near_copies(member):
            copy.start()
    for flip in (1, 2):
        for copy in far_copies(flip):
            copy.start()
    for item in range(more):
        tok[0](item)
    for item in range(count):
        grp[0](item)
    for copy in masks:
        copy.wait()
    mask_rows(seg_buf, mask_buf, count_ref, bias)

    def compute(step):
        member, flip = slot_of(step)
        slot = 4 * member + flip

        @pl.when(step < 2)
        def _():
            for copy in tok_copies(member):
                copy.wait()
            dk[member] = jnp.zeros((TOK_DEV, D), F32)
            dv[member] = jnp.zeros((TOK_DEV, D), F32)

        loads(step).wait()

        @pl.when(step + 3 < 4 * MB)
        def _():
            loads(step + 3).start()

        @pl.when(flip == 0)
        def _():
            for copy in own_copies(member):
                copy.wait()
            for copy in near_copies(member):
                copy.wait_recv()

        @pl.when(flip > 0)
        def _():
            for copy in on_copies(slot):
                copy.wait_recv()

        asked = queries[lax.rem(step, 4)]
        upstream = ups[slot].reshape(span, D)
        scores = nt(asked, keys[member])
        soft = nt(upstream, values[member])
        weights, grads = [], []
        for half in range(2):
            seen = bias[member, pl.ds(2 * chip_at(chip, flip) + half, 1), :]
            figures = figs[slot, half].T
            rows = slice(half * ROWS, (half + 1) * ROWS)
            weight = jnp.exp2(scores[rows] + seen - figures[:, 0:1])
            grads.append((weight * (soft[rows] - figures[:, 1:2])).astype(BF16))
            weights.append(weight.astype(BF16))
        weight = jnp.concatenate(weights, axis=0)
        grad = jnp.concatenate(grads, axis=0)
        dv[member] += tn(weight, upstream)
        dk[member] += tn(grad, asked)
        asked_grad = (nn(grad, keys[member]) * D ** (-0.5)).astype(BF16)

        @pl.when(step >= 4)
        def _():
            core_copy(step - 4).wait_send()

        for half in range(2):
            part[lax.rem(step, 4), half] = asked_grad[half * ROWS:(half + 1) * ROWS]
        core_copy(step).start()

    def combine(step):
        member, flip = slot_of(step)
        slot = 4 * member + flip
        core_copy(step).wait_recv()
        added = part[lax.rem(step, 4), core].astype(F32) + got[slot].astype(F32)

        @pl.when(flip > 0)
        def _():
            stage[slot] = added.astype(BF16)

        @pl.when(flip == 0)
        def _():
            total[member] = added

    def tokens_back(member, half):
        gain = tgain_ref[...]
        rows = pl.ds(pl.multiple_of(half * span, span), span)
        hat, inverse = norm_parts(tok_buf[member, rows].astype(F32))
        normed = (hat * gain).astype(BF16)
        key_grad = (dk[member, rows] * LN2).astype(BF16)
        value_grad = dv[member, rows].astype(BF16)
        dkw[...] += tn(normed, key_grad)
        dvw[...] += tn(normed, value_grad)
        normed_grad = nt(key_grad, kw_ref[...]) + nt(value_grad, vw_ref[...])
        source_grad, gain_rows = norm_pull(hat, inverse, gain, normed_grad)
        dk[member, rows] = source_grad
        dgain_ref[...] += jnp.sum(gain_rows, axis=0, keepdims=True)

    def hold(item):
        helds[item][...] = tok[4](item).astype(helds[item].dtype)

    def step_body(step, carry):
        compute(step)

        @pl.when(step > 0)
        def _():
            combine(step - 1)

        @pl.when(step == 0)
        def _():
            for flip in (1, 2):
                for copy in far_copies(4 + flip):
                    copy.start()
            tok[1](0)

        @pl.when(step == 1)
        def _():
            pass_near(0)

        @pl.when(step == 2)
        def _():
            tok[1](1)

        @pl.when(step == 3)
        def _():
            pass_on(3)
            pass_near(1)

        @pl.when(step == 4)
        def _():
            pass_on(7)
            for item in range(count):
                grp[4](item)
            tok[1](2)

        @pl.when(step == 5)
        def _():
            for copy in half_copies(0):
                copy.start()
            tok[2](0)

        @pl.when(step == 6)
        def _():
            for copy in half_copies(1):
                copy.start()
            relay(0)

        @pl.when(step == 4 * MB - 1)
        def _():
            tok[3](0)
            tok[2](1)

        return carry

    lax.fori_loop(0, 4 * MB, step_body, 0)

    def tokens_body(member, carry):
        @pl.when(member == 1)
        def _():
            hold(0)
            tok[2](2)

        for half in range(TOK_DEV // span):
            tokens_back(member, half)
        out_copy(member).start()

        @pl.when(member == 0)
        def _():
            combine(4 * MB - 1)
            relay(1)

        return carry

    dkw[...] = jnp.zeros_like(dkw)
    dvw[...] = jnp.zeros_like(dvw)
    dgain_ref[...] = jnp.zeros_like(dgain_ref)
    lax.fori_loop(0, MB, tokens_body, 0)
    dkw_ref[...] = dkw[...].astype(BF16)
    dvw_ref[...] = dvw[...].astype(BF16)
    tok[3](1)
    tok[3](2)
    for copy in tails:
        copy.wait()
    gain = qgain_ref[...]
    hat, inverse = norm_parts(lat[...].reshape(MB * ROWS, D))
    normed = (hat * gain).astype(BF16)
    asked_grads = []
    for member in range(MB):
        added = total[member]
        for flip in (1, 2):
            chip_copy(4 * member + flip).wait_recv()
            added = added + arrive[2 * member + flip - 1].astype(F32)
        asked_grads.append(added.astype(BF16))
    asked_grad = jnp.concatenate(asked_grads, axis=0)
    dqw_ref[...] = tn(normed, asked_grad).astype(BF16)
    source_grad, gain_rows = norm_pull(hat, inverse, gain, nt(asked_grad, qw_ref[...]))
    lup[...] += source_grad
    last = pltpu.make_async_copy(lup, dlat_ref, tail_sem.at[2])
    last.start()
    query_gain = jnp.sum(gain_rows, axis=0, keepdims=True)
    rows = jnp.concatenate(
        [dgain_ref[...], query_gain, fgain_ref[...], mgain_ref[...], sgain_ref[...], jnp.zeros((3, D), F32)], axis=0
    )
    gains_ref[...] = jnp.zeros_like(gains_ref)
    width = D // TOK
    for device in range(TOK):
        gains_ref[16 * device:16 * device + 8, 0:width] = rows[:, device * width:(device + 1) * width]
    grp[3]((0,))
    hold(1)
    hold(2)
    tok[5]()
    last.wait()
    for step in range(4, 4 * MB):
        core_copy(jnp.int32(step)).wait_send()
    for member in range(MB):
        out_copy(member).wait()
        for copy in near_copies(member) + half_copies(member):
            copy.wait_send()
        for flip in range(4):
            slot = 4 * member + flip
            if flip > 0:
                for copy in far_copies(slot):
                    copy.wait_send()
                for copy in on_copies(slot):
                    copy.wait_send()
            if flip in (1, 2):
                chip_copy(slot).wait_send()


CROSS_SCRATCH = 44


def cross_backward(collective_id, arrays, grads, *args):
    dma = pltpu.SemaphoreType.DMA
    span = 2 * ROWS
    steps = 4 * MB
    vmem = pl.BlockSpec(memory_space=pltpu.VMEM)
    hbm = pl.BlockSpec(memory_space=pl.ANY)
    smem = pl.BlockSpec(memory_space=pltpu.SMEM)
    items, kinds = held_plan(arrays)
    sources, grad_items, grad_kinds, shapes = reduce_plan(grads)
    scratch = [
        pltpu.VMEM((MB, TOK_DEV, D), BF16),
        pltpu.VMEM((MB, TOK_DEV, D), BF16),
        pltpu.VMEM((MB, TOK_DEV, D), BF16),
        pltpu.VMEM((4, span, D), BF16),
        pltpu.VMEM((steps, 2, ROWS, D), BF16),
        pltpu.VMEM((steps, 2, 8, ROWS), F32),
        pltpu.VMEM((MB, LGROUPS, TOK_DEV), F32),
        pltpu.VMEM((4, 2, ROWS, D), BF16),
        pltpu.VMEM((steps, ROWS, D), BF16),
        pltpu.VMEM((steps, ROWS, D), BF16),
        pltpu.VMEM((2 * MB, ROWS, D), BF16),
        pltpu.VMEM((MB, 2, ROWS // 2, D), BF16),
        pltpu.VMEM((MB, ROWS, D), F32),
        pltpu.VMEM((MB, TOK_DEV, D), F32),
        pltpu.VMEM((MB, TOK_DEV, D), F32),
        pltpu.VMEM((D, D), F32),
        pltpu.VMEM((D, D), F32),
        pltpu.VMEM((1, D), F32),
        pltpu.VMEM((MB, ROWS, D), F32),
        pltpu.VMEM((MB * ROWS, D), F32),
        pltpu.VMEM((MB, TOK_DEV), jnp.int32),
        pltpu.VMEM((MB, SCENES, LGROUPS), jnp.int32),
        dma((2,)), dma((3,)),
        dma((MB,)), dma((MB,)), dma((MB,)), dma((4,)), dma((MB,)),
        dma((MB, 2)), dma((MB, 2)), dma((steps, 2)), dma((steps, 2)), dma((steps, 2)), dma((steps, 2)), dma((MB, 2)),
        dma((MB,)), dma((MB,)),
        dma((steps,)), dma((steps,)), dma((2 * MB,)), dma((2 * MB,)), dma((MB, 2)), dma((MB, 2)),
    ]
    return pl.pallas_call(
        functools.partial(cross_backward_kernel, items, grad_items),
        in_specs=[hbm] + [vmem] * 3 + [hbm, hbm, smem] + [hbm] * 7 + [vmem] * 5 + [vmem] * len(arrays) + [hbm] * len(grads),
        out_specs=[hbm, hbm] + [vmem] * (4 + len(arrays) + len(grads)),
        out_shape=[
            jax.ShapeDtypeStruct((MB * ROWS, D), F32),
            jax.ShapeDtypeStruct((1, MB, TOK_DEV, D), F32),
            jax.ShapeDtypeStruct((D, D), BF16),
            jax.ShapeDtypeStruct((D, D), BF16),
            jax.ShapeDtypeStruct((D, D), BF16),
            jax.ShapeDtypeStruct((16 * TOK, 128), F32),
        ] + [jax.ShapeDtypeStruct(array.shape, array.dtype) for array in arrays]
        + [jax.ShapeDtypeStruct((high // 2, wide), kind) for (high, wide), kind in zip(shapes, grad_kinds)],
        scratch_shapes=scratch + grp_scratch(items, kinds) + tok_scratch(grad_items, grad_kinds),
        compiler_params=pltpu.CompilerParams(
            collective_id=collective_id, has_side_effects=True, vmem_limit_bytes=60 * MIB
        ),
        cost_estimate=pl.CostEstimate(
            flops=26 * 10**9, bytes_accessed=24 * 10**6, transcendentals=4 * 10**6
        ),
        name="cross_backward",
    )(*args, *arrays, *sources)


GELU_A = 0.7978845608028654
GELU_B = 0.044715


def gelu_parts(hidden):
    square = hidden * hidden
    bent = jnp.tanh(GELU_A * hidden * (1.0 + GELU_B * square))
    half = 0.5 * (1.0 + bent)
    slope = half + 0.5 * hidden * (1.0 - bent * bent) * (GELU_A * (1.0 + 3.0 * GELU_B * square))
    return hidden * half, slope


def greet_all(tok_devices, grp_devices=()):
    barrier = pltpu.get_barrier_semaphore()
    for axis, devices in (("tok", tok_devices), ("grp", grp_devices)):
        for device in devices:
            pl.semaphore_signal(
                barrier, inc=1, device_id={axis: device}, device_id_type=pl.DeviceIdType.MESH
            )
    pl.semaphore_wait(barrier, len(tok_devices) + len(grp_devices))


def all_peers():
    me, core, chip, mate, others = places()
    peers = []
    for other in others:
        peers += [2 * other + core, 2 * other + 1 - core]
    return me, peers + [mate]


def head_copies(row_side, head_side, to_heads, member, me, peers, send, recv, local):
    lanes = pl.ds(member * ROWS, ROWS)
    row_at = lambda device: row_side.at[:, device, :, lanes]
    head_at = lambda device: head_side.at[:, member, :, pl.ds(pl.multiple_of(device * ROWS, ROWS), ROWS)]
    source, target = (row_at, head_at) if to_heads else (head_at, row_at)
    copies = [
        remote(source(peer), target(me), send.at[slot, member], recv.at[slot, member], peer)
        for slot, peer in enumerate(peers)
    ]
    return copies, pltpu.make_async_copy(source(me), target(me), local.at[member])


QB = 1024
QB_BACK = 256


def latents_forward_kernel(
    lat_ref, att_ref, cot_ref, ow_ref, fgain_ref, fup_ref, fdown_ref, mgain_ref, proj_ref, mow_ref, sgain_ref,
    sup_ref, sdown_ref,
    out_ref, fmid_ref, mmid_ref, packed_ref, exact_ref, lse_ref, up_ref, mgrad_ref, ddown_ref, dup_ref, dmo_ref,
    dgain_ref,
    lat, att, cot, ow, fup, fdown, proj, mow, sup, sdown,
    out, fmid, mmid, heads, exact, up, mgrad, ddown, dup, dmo,
    rows_out, keys, values, mixed, mixed_rows,
    load_sem, store_sem, send_a, recv_a, local_a, send_b, recv_b, local_b,
):
    me, peers = all_peers()
    own = pl.ds(pl.multiple_of(me * ROWS, ROWS), ROWS)
    names = ("lat", "att", "ow", "fup", "fdown", "proj", "mow", "sup", "sdown", "cot")
    loads = {}
    for i, (source, target) in enumerate((
        (lat_ref.at[0, :, own], lat), (att_ref, att), (ow_ref, ow), (fup_ref, fup), (fdown_ref, fdown),
        (proj_ref, proj), (mow_ref, mow), (sup_ref, sup), (sdown_ref, sdown), (cot_ref.at[0], cot),
    )):
        loads[names[i]] = pltpu.make_async_copy(source, target, load_sem.at[i])
        loads[names[i]].start()
    stores = []

    def store(source, target):
        stores.append(pltpu.make_async_copy(source, target, store_sem.at[len(stores)]))
        stores[-1].start()

    greet_all(peers)
    flat = (MB * ROWS, D)
    for name in ("lat", "att", "ow"):
        loads[name].wait()
    first = lat[...].reshape(flat) + nn(att[...].reshape(flat).astype(BF16), ow[...])
    fmid[...] = first
    store(fmid, fmid_ref)
    normed = (norm_parts(first)[0] * fgain_ref[...]).astype(BF16)
    loads["fup"].wait()
    loads["fdown"].wait()
    mid = first
    for part in range(2):
        cut = slice(part * FF // 2, (part + 1) * FF // 2)
        mid = mid + nn(jax.nn.gelu(nn(normed, fup[:, cut])).astype(BF16), fdown[cut])
    mmid[...] = mid
    store(mmid, mmid_ref)
    normed = (norm_parts(mid)[0] * mgain_ref[...]).astype(BF16).T
    loads["proj"].wait()
    for kind, scale in enumerate((HD ** (-0.5) * LOG2E, 1.0, 1.0)):
        packed = tn(proj[:, kind * D:(kind + 1) * D], normed) * scale
        rows_out[kind] = packed.astype(BF16).reshape(H, HD, MB * ROWS)
    outward = [head_copies(rows_out, heads, True, member, me, peers, send_a, recv_a, local_a) for member in range(MB)]
    backward = [
        head_copies(mixed_rows, mixed, False, member, me, peers, send_b, recv_b, local_b) for member in range(MB)
    ]
    for copies, here in outward:
        for copy in copies:
            copy.start()
        here.start()
    for member in range(MB):
        copies, here = outward[member]
        for copy in copies:
            copy.wait_recv()
        here.wait()
        store(heads.at[:, member], packed_ref.at[:, member])
        keys[...] = heads[1, member].T
        values[0:HD] = heads[2, member]
        values[HD:] = jnp.ones((16, L), BF16)

        def attend(step, carry, member=member):
            at = pl.ds(pl.multiple_of(step * QB, QB), QB)
            logits = nn(keys[...], heads[0, member, :, at])
            top = jnp.max(logits, axis=0, keepdims=True)
            both = nn(values[...], jnp.exp2(logits - top).astype(BF16))
            total = both[HD:HD + 1]
            result = both[0:HD] / total
            exact[member, :, at] = result
            mixed[0, member, :, at] = result.astype(BF16)
            lse_ref[member, :, at] = jnp.broadcast_to(top + jnp.log2(total), (8, QB))
            return carry

        lax.fori_loop(0, L // QB, attend, 0)
        for copy in backward[member][0] + [backward[member][1]]:
            copy.start()
    store(exact, exact_ref)
    loads["mow"].wait()
    loads["sup"].wait()
    loads["sdown"].wait()
    loads["cot"].wait()
    for copies, here in backward:
        for copy in copies:
            copy.wait_recv()
        here.wait()
    mixed_t = mixed_rows[0].reshape(D, MB * ROWS)
    second = mmid[...] + tn(mixed_t, mow[...])
    hat, inverse = norm_parts(second)
    normed = (hat * sgain_ref[...]).astype(BF16)
    upstream = cot[...].reshape(flat)
    grad = upstream.astype(BF16)
    final = second
    normed_grad = jnp.zeros(flat, F32)
    for part in range(2):
        cut = slice(part * FF // 2, (part + 1) * FF // 2)
        act, slope = gelu_parts(nn(normed, sup[:, cut]))
        act = act.astype(BF16)
        final = final + nn(act, sdown[cut])
        hidden_grad = (slope * nt(grad, sdown[cut])).astype(BF16)
        normed_grad = normed_grad + nt(hidden_grad, sup[:, cut])
        ddown[cut] = tn(act, grad).astype(BF16)
        dup[:, cut] = tn(normed, hidden_grad).astype(BF16)
    store(ddown, ddown_ref)
    store(dup, dup_ref)
    out[...] = final.reshape(MB, ROWS, D)
    store(out, out_ref.at[0])
    residual, gain_rows = norm_pull(hat, inverse, sgain_ref[...], normed_grad)
    dgain_ref[...] = jnp.sum(gain_rows, axis=0, keepdims=True)
    upstream = upstream + residual
    up[...] = upstream
    store(up, up_ref)
    grad = upstream.astype(BF16)
    mgrad[0] = nt(mow[...], grad).astype(BF16).reshape(H, HD, MB * ROWS)
    store(mgrad, mgrad_ref)
    dmo[...] = nn(mixed_t, grad).astype(BF16)
    store(dmo, dmo_ref)
    for copy in stores:
        copy.wait()
    for copies, here in outward + backward:
        for copy in copies:
            copy.wait_send()


def latents_forward(collective_id, *args):
    dma = pltpu.SemaphoreType.DMA
    vmem = pl.BlockSpec(memory_space=pltpu.VMEM)
    hbm = pl.BlockSpec(memory_space=pl.ANY)
    rows = MB * ROWS
    stored = [
        ((1, MB, ROWS, D), F32), ((rows, D), F32), ((rows, D), F32), ((3, MB, HD, L), BF16), ((MB, HD, L), F32),
        ((MB, 8, L), F32), ((rows, D), F32), ((1, H, HD, rows), BF16), ((FF, D), BF16), ((D, FF), BF16), ((D, D), BF16),
        ((1, D), F32),
    ]
    return pl.pallas_call(
        latents_forward_kernel,
        in_specs=[hbm, hbm, hbm, hbm, vmem, hbm, hbm, vmem, hbm, hbm, vmem, hbm, hbm],
        out_specs=[hbm] * 5 + [vmem] + [hbm] * 5 + [vmem],
        out_shape=[jax.ShapeDtypeStruct(shape, kind) for shape, kind in stored],
        scratch_shapes=[
            pltpu.VMEM((MB, ROWS, D), F32), pltpu.VMEM((MB, ROWS, D), F32), pltpu.VMEM((MB, ROWS, D), F32),
            pltpu.VMEM((D, D), BF16), pltpu.VMEM((D, FF), BF16), pltpu.VMEM((FF, D), BF16),
            pltpu.VMEM((D, 3 * D), BF16), pltpu.VMEM((D, D), BF16), pltpu.VMEM((D, FF), BF16),
            pltpu.VMEM((FF, D), BF16),
            pltpu.VMEM((MB, ROWS, D), F32), pltpu.VMEM((rows, D), F32), pltpu.VMEM((rows, D), F32),
            pltpu.VMEM((3, MB, HD, L), BF16), pltpu.VMEM((MB, HD, L), F32), pltpu.VMEM((rows, D), F32),
            pltpu.VMEM((1, H, HD, rows), BF16), pltpu.VMEM((FF, D), BF16), pltpu.VMEM((D, FF), BF16),
            pltpu.VMEM((D, D), BF16),
            pltpu.VMEM((3, H, HD, rows), BF16), pltpu.VMEM((L, HD), BF16), pltpu.VMEM((HD + 16, L), BF16),
            pltpu.VMEM((1, MB, HD, L), BF16), pltpu.VMEM((1, H, HD, rows), BF16),
            dma((10,)), dma((11,)), dma((7, MB)), dma((7, MB)), dma((MB,)), dma((7, MB)), dma((7, MB)), dma((MB,)),
        ],
        compiler_params=pltpu.CompilerParams(
            collective_id=collective_id, has_side_effects=True, vmem_limit_bytes=60 * MIB
        ),
        cost_estimate=pl.CostEstimate(
            flops=20 * 10**9, bytes_accessed=30 * 10**6, transcendentals=10 * 10**6
        ),
        name="latents_forward",
    )(*args)


def levels():
    level = lax.axis_index("grp")
    odd = lax.rem(level, 2)
    return odd, level + 1 - 2 * odd, lax.rem(level + 2, 4)


def half_slices(rows, odd):
    half = rows // 2
    keep = pl.ds(pl.multiple_of(odd * half, half), half)
    away = pl.ds(pl.multiple_of((1 - odd) * half, half), half)
    return keep, away


def tok_steps(items, sources, scratch):
    n = len(items)
    mine, got, near_in, first_in, second_in = [scratch[i * n:(i + 1) * n] for i in range(5)]
    (local_sem, core_send, core_recv, near_send, near_recv, one_send, one_recv, two_send, two_recv) = scratch[5 * n:]
    me, core, chip, mate, (far, flip_x, flip_y) = places()
    x, y = lax.rem(chip, 2), lax.div(chip, 2)
    odd, level_near, level_far = levels()

    def core_copies(i):
        source, rows, row_at, columns, column_at, x_first = items[i]
        part = (pl.ds(row_at, rows), pl.ds(column_at, columns))
        return (
            remote(sources[source].at[:, :, 1 - core, *part], got[i], core_send.at[i], core_recv.at[i], mate),
            pltpu.make_async_copy(sources[source].at[:, :, core, *part], mine[i], local_sem.at[i]),
        )

    def near_copy(i):
        keep, away = half_slices(items[i][1], odd)
        return pltpu.make_async_remote_copy(
            src_ref=mine[i].at[:, :, away], dst_ref=near_in[i], send_sem=near_send.at[i], recv_sem=near_recv.at[i],
            device_id={"grp": level_near}, device_id_type=pl.DeviceIdType.MESH,
        )

    def first_copy(i):
        keep, away = half_slices(items[i][1], odd)
        x_first = items[i][-1]
        source = mine[i].at[:, 1 - x, keep] if x_first else mine[i].at[1 - y, :, keep]
        peer = 2 * (flip_x if x_first else flip_y) + core
        return remote(source, first_in[i], one_send.at[i], one_recv.at[i], peer)

    def second_copy(i):
        keep, away = half_slices(items[i][1], odd)
        x_first = items[i][-1]
        source = mine[i].at[1 - y, x, keep] if x_first else mine[i].at[y, 1 - x, keep]
        peer = 2 * (flip_y if x_first else flip_x) + core
        return remote(source, second_in[i], two_send.at[i], two_recv.at[i], peer)

    def core_sends(i):
        for copy in core_copies(i):
            copy.start()

    def core_sums(i):
        there, here = core_copies(i)
        there.wait_recv()
        here.wait()
        add(mine[i], mine[i], got[i])
        near_copy(i).start()

    def near_sums(i):
        keep, away = half_slices(items[i][1], odd)
        near_copy(i).wait_recv()
        held = mine[i].at[:, :, keep]
        add(held, held, near_in[i])
        first_copy(i).start()

    def first_sums(i):
        keep, away = half_slices(items[i][1], odd)
        first_copy(i).wait_recv()
        held = mine[i].at[:, x, keep] if items[i][-1] else mine[i].at[y, :, keep]
        add(held, held, first_in[i])
        second_copy(i).start()

    def second_sums(i):
        keep, away = half_slices(items[i][1], odd)
        second_copy(i).wait_recv()
        return mine[i][y, x, keep].astype(F32) + second_in[i][...].astype(F32)

    def finish():
        for i in range(n):
            core_copies(i)[0].wait_send()
            for copy in (near_copy(i), first_copy(i), second_copy(i)):
                copy.wait_send()

    return (core_sends, core_sums, near_sums, first_sums, second_sums, finish), (
        mate, 2 * flip_x + core, 2 * flip_y + core)


def plain_steps(items, sources, scratch):
    n = len(items)
    mine, got, near_in, first_in, second_in = [scratch[i * n:(i + 1) * n] for i in range(5)]
    (local_sem, core_send, core_recv, near_send, near_recv, one_send, one_recv, two_send, two_recv) = scratch[5 * n:]
    me, core, chip, mate, (far, flip_x, flip_y) = places()
    x, y = lax.rem(chip, 2), lax.div(chip, 2)
    odd, level_near, level_far = levels()

    def core_copy(i):
        return remote(sources[i].at[:, :, 1 - core], got[i], core_send.at[i], core_recv.at[i], mate)

    def local_copy(i):
        return pltpu.make_async_copy(sources[i].at[:, :, core], mine[i], local_sem.at[i])

    def first_copy(i):
        x_first = items[i][-1]
        source = mine[i].at[:, 1 - x] if x_first else mine[i].at[1 - y]
        peer = 2 * (flip_x if x_first else flip_y) + core
        return remote(source, first_in[i], one_send.at[i], one_recv.at[i], peer)

    def second_copy(i):
        x_first = items[i][-1]
        source = mine[i].at[1 - y, x] if x_first else mine[i].at[y, 1 - x]
        peer = 2 * (flip_y if x_first else flip_x) + core
        return remote(source, second_in[i], two_send.at[i], two_recv.at[i], peer)

    def near_copy(i):
        keep, away = half_slices(items[i][1], odd)
        return pltpu.make_async_remote_copy(
            src_ref=mine[i].at[y, x, away], dst_ref=near_in[i], send_sem=near_send.at[i], recv_sem=near_recv.at[i],
            device_id={"grp": level_near}, device_id_type=pl.DeviceIdType.MESH,
        )

    def core_sends(i):
        core_copy(i).start()
        local_copy(i).start()

    def core_sums(i):
        core_copy(i).wait_recv()
        local_copy(i).wait()
        add(mine[i], mine[i], got[i])
        first_copy(i).start()

    def first_sums(i):
        first_copy(i).wait_recv()
        held = mine[i].at[:, x] if items[i][-1] else mine[i].at[y]
        add(held, held, first_in[i])
        second_copy(i).start()

    def second_sums(i):
        second_copy(i).wait_recv()
        held = mine[i].at[y, x]
        add(held, held, second_in[i])
        near_copy(i).start()

    def near_sums(i):
        keep, away = half_slices(items[i][1], odd)
        near_copy(i).wait_recv()
        return mine[i][y, x, keep].astype(F32) + near_in[i][...].astype(F32)

    def finish():
        for i in range(n):
            for copy in (core_copy(i), near_copy(i), first_copy(i), second_copy(i)):
                copy.wait_send()

    return (core_sends, core_sums, first_sums, second_sums, near_sums, finish), (
        mate, 2 * flip_x + core, 2 * flip_y + core)


def grp_steps(items, held, outs, scratch, joined=None):
    n = len(items)
    far_in, own_joined, near_in = [scratch[i * n:(i + 1) * n] for i in range(3)]
    z_send, z_recv = scratch[3 * n:]
    joined = own_joined if joined is None else joined
    odd, level_near, level_far = levels()

    def along(i, step):
        source, target, other = (
            (held[i], far_in[i], level_far),
            (joined[i], near_in[i], level_near),
        )[step]
        return pltpu.make_async_remote_copy(
            src_ref=source, dst_ref=target, send_sem=z_send.at[i, step], recv_sem=z_recv.at[i, step],
            device_id={"grp": other}, device_id_type=pl.DeviceIdType.MESH,
        )

    def store(i, odd_half, value):
        source, rows, row_at, columns, column_at, x_first = items[i]
        half = rows // 2
        start = pl.multiple_of(row_at + odd_half * half, half)
        outs[source][pl.ds(start, half), pl.ds(column_at, columns)] = value.astype(F32)

    def far_start(i):
        along(i, 0).start()

    def far_join(i):
        along(i, 0).wait_recv()
        add(joined[i], held[i], far_in[i])

    def near_start(i):
        along(i, 1).start()
        store(i, odd, joined[i][...])

    def far_sum(i):
        far_join(i)
        near_start(i)

    def near_store(i):
        along(i, 1).wait_recv()
        store(i, 1 - odd, near_in[i][...])

    def finish(steps=(0, 1)):
        for i in range(n):
            for step in steps:
                along(i, step).wait_send()

    return (far_start, far_sum, near_store, finish, far_join, near_start), (level_near, level_far)


def add(target, one, two):
    target[...] = (one[...].astype(F32) + two[...].astype(F32)).astype(target.dtype)


def reduce_kernel(items, whole, joined, count, *refs):
    n, m, k = len(items), len(whole), len(joined)
    sources, held, done = refs[:count], refs[count:count + m], refs[count + m:count + m + k]
    refs = refs[count + m + k:]
    outs, whole_outs, joined_outs = refs[:count], refs[count:count + m], refs[count + m:count + m + k]
    scratch = refs[count + m + k:]
    cut = 5 * n + 9
    own_held = scratch[cut:cut + n]
    tok, near_devices = plain_steps(items, sources, scratch[:cut])
    cut += n
    late, grp_devices = grp_steps(items, own_held, outs, scratch[cut:cut + 3 * n + 2])
    cut += 3 * n + 2
    early, unused = grp_steps(whole, held, whole_outs, scratch[cut:cut + 3 * m + 2])
    cut += 3 * m + 2
    first, unused = grp_steps(joined, done, joined_outs, scratch[cut:], done)
    greet_all(near_devices, grp_devices)
    for i in range(n):
        tok[0](i)
    for i in range(m):
        early[0](i)
    for i in range(n):
        tok[1](i)
    for i in range(k):
        first[5](i)
    for i in range(n):
        tok[2](i)
    early[1](0)
    for i in range(n):
        tok[3](i)
    for i in range(n):
        own_held[i][...] = tok[4](i).astype(own_held[i].dtype)
        late[0](i)
    for i in range(1, m):
        early[1](i)
        early[2](i - 1)
    for i in range(k):
        first[2](i)
    for i in range(n):
        late[1](i)
    early[2](m - 1)
    for i in range(n):
        late[2](i)
    tok[-1]()
    late[3]()
    early[3]()
    first[3]((1,))


def reduce_plan(arrays):
    sources, items = [], []
    for source, array in enumerate(arrays):
        rows, columns = array.shape[0] // TOK, array.shape[1]
        sources.append(array.reshape(2, 2, 2, rows, columns))
        items.append((source, rows, 0, columns, 0, source % 2 == 0))
    kinds = [array.dtype for array in arrays]
    shapes = [(array.shape[0] // TOK, array.shape[1]) for array in arrays]
    return sources, tuple(items), kinds, shapes


def held_plan(arrays):
    items = tuple((i, 2 * array.shape[0], 0, array.shape[1], 0, True) for i, array in enumerate(arrays))
    return items, [array.dtype for array in arrays]


def item_blocks(items, kinds, lead, part):
    return [pltpu.VMEM(lead + (item[1] // part, item[3]), kind) for item, kind in zip(items, kinds)]


def plain_scratch(items, kinds):
    blocks = functools.partial(item_blocks, items, kinds)
    return (blocks((2, 2), 1) + blocks((2, 2), 1) + blocks((), 2) + blocks((2,), 1) + blocks((), 1)
            + [pltpu.SemaphoreType.DMA((len(items),))] * 9)


def tok_scratch(items, kinds):
    blocks = functools.partial(item_blocks, items, kinds)
    return (blocks((2, 2), 1) + blocks((2, 2), 1) + blocks((2, 2), 2) + blocks((2,), 2) + blocks((), 2)
            + [pltpu.SemaphoreType.DMA((len(items),))] * 9)


def grp_scratch(items, kinds):
    blocks = functools.partial(item_blocks, items, kinds)
    return blocks((), 2) * 3 + [pltpu.SemaphoreType.DMA((len(items), 2))] * 2


def reduce_grads(collective_id, arrays, held, done):
    sources, items, kinds, shapes = reduce_plan(arrays)
    whole, whole_kinds = held_plan(held)
    joined, joined_kinds = held_plan(done)
    vmem = pl.BlockSpec(memory_space=pltpu.VMEM)
    hbm = pl.BlockSpec(memory_space=pl.ANY)
    return pl.pallas_call(
        functools.partial(reduce_kernel, items, whole, joined, len(arrays)),
        in_specs=[hbm] * len(arrays) + [vmem] * (len(held) + len(done)),
        out_specs=[vmem] * (len(arrays) + len(held) + len(done)),
        out_shape=[jax.ShapeDtypeStruct(shape, F32) for shape in shapes]
        + [jax.ShapeDtypeStruct((item[1], item[3]), F32) for item in whole + joined],
        scratch_shapes=plain_scratch(items, kinds) + item_blocks(items, kinds, (), 2) + grp_scratch(items, kinds)
        + grp_scratch(whole, whole_kinds) + grp_scratch(joined, joined_kinds),
        compiler_params=pltpu.CompilerParams(
            collective_id=collective_id, has_side_effects=True, vmem_limit_bytes=56 * MIB
        ),
        name="reduce_grads",
    )(*sources, *held, *done)


def write_kernel(count, *refs):
    sources, gain_ref, outs = refs[:count], refs[count], refs[count + 1:2 * count + 1]
    gain_outs, buffers = refs[2 * count + 1:-count - 2], refs[-count - 2:-2]
    in_sem, out_sem = refs[-2:]
    ins = [pltpu.make_async_copy(sources[i], buffers[i], in_sem.at[i]) for i in range(count)]
    backs = [pltpu.make_async_copy(buffers[i], outs[i], out_sem.at[i]) for i in range(count)]
    for copy in ins:
        copy.start()
    for i, out in enumerate(gain_outs):
        out[...] = gain_ref[i:i + 1, 0:D // TOK]
    for i in range(count):
        ins[i].wait()
        backs[i].start()
    for copy in backs:
        copy.wait()


def write_results(results, gains, gain_count):
    n = len(results)
    hbm, vmem = pl.BlockSpec(memory_space=pl.ANY), pl.BlockSpec(memory_space=pltpu.VMEM)
    return pl.pallas_call(
        functools.partial(write_kernel, n),
        in_specs=[hbm] * n + [vmem],
        out_specs=[hbm] * n + [vmem] * gain_count,
        out_shape=[jax.ShapeDtypeStruct(result.shape, result.dtype) for result in results]
        + [jax.ShapeDtypeStruct((1, D // TOK), F32)] * gain_count,
        scratch_shapes=[pltpu.VMEM(result.shape, result.dtype) for result in results]
        + [pltpu.SemaphoreType.DMA((n,)), pltpu.SemaphoreType.DMA((n,))],
        compiler_params=pltpu.CompilerParams(vmem_limit_bytes=60 * MIB),
        name="write_results",
    )(*results, gains)


def latents_backward_kernel(items, *refs):
    (mgrad_ref, packed_ref, exact_ref, lse_ref, up_ref, mmid_ref, fmid_ref, att_ref, clse_ref, ow_ref, fgain_ref,
     fup_ref, fdown_ref, mgain_ref, proj_ref) = refs[:15]
    count = max(item[0] for item in items) + 1
    sources = refs[15:15 + count]
    (agrad_ref, fig_ref, lup_ref, dup_ref, ddown_ref, dproj_ref, dout_ref, dmgain_ref, dfgain_ref) = refs[
        15 + count:24 + count]
    reduced = refs[24 + count:24 + 2 * count]
    rest = refs[24 + 2 * count:]
    (heads, exact, ups, mmid, fmid, att, ow, fup, fdown, proj, keys, values, upstream_heads, key_acc, value_acc,
     grads, back, agrad, lup, dup, ddown, dproj, dout, hidden,
     load_sem, store_sem, send_a, recv_a, local_a, send_b, recv_b, local_b) = rest[:32]
    me, peers = all_peers()
    reducer, near_devices = tok_steps(items, sources, rest[32:])
    core_sends, core_sums, near_sums, first_sums, second_sums, finish = reducer
    odd, level_near, level_far = levels()

    def hold(item):
        reduced[item][...] = second_sums(item).astype(reduced[item].dtype)

    names = ("heads", "exact", "fmid", "fup", "up", "mmid", "proj", "fdown", "att", "ow")
    loads = {}
    for i, (source, target) in enumerate((
        (packed_ref, heads), (exact_ref, exact), (fmid_ref, fmid), (fup_ref, fup), (up_ref, ups), (mmid_ref, mmid),
        (proj_ref, proj), (fdown_ref, fdown), (att_ref, att), (ow_ref, ow),
    )):
        loads[names[i]] = pltpu.make_async_copy(source, target, load_sem.at[i])
        loads[names[i]].start()
    stores = []

    def store(source, target):
        stores.append(pltpu.make_async_copy(source, target, store_sem.at[len(stores)]))
        stores[-1].start()

    greet_all(peers, (level_near,))
    outward = [
        head_copies(mgrad_ref, upstream_heads, True, member, me, peers, send_a, recv_a, local_a) for member in range(MB)
    ]
    backward = [head_copies(back, grads, False, member, me, peers, send_b, recv_b, local_b) for member in range(MB)]
    for copies, here in outward:
        for copy in copies:
            copy.start()
        here.start()
    for item in range(3):
        core_sends(item)
    loads["fmid"].wait()
    loads["fup"].wait()
    first_hat, first_inverse = norm_parts(fmid[...])
    first_normed = (first_hat * fgain_ref[...]).astype(BF16)
    hidden[...] = nn(first_normed, fup[...])
    core_sums(0)
    loads["heads"].wait()
    loads["exact"].wait()
    for member in range(MB):
        keys[...] = heads[1, member].T
        values[...] = heads[2, member].T
        key_acc[...] = jnp.zeros_like(key_acc)
        value_acc[...] = jnp.zeros_like(value_acc)
        copies, here = outward[member]
        for copy in copies:
            copy.wait_recv()
        here.wait()

        def attend_back(step, carry, member=member):
            at = pl.ds(pl.multiple_of(step * QB_BACK, QB_BACK), QB_BACK)
            queries = heads[0, member, :, at]
            upstream = upstream_heads[0, member, :, at]
            inner = jnp.sum(upstream.astype(F32) * exact[member, :, at], axis=0, keepdims=True)
            softened = jnp.exp2(nn(keys[...], queries) - lse_ref[member, 0:1, at])
            logit_grad = (softened * (nn(values[...], upstream) - inner)).astype(BF16)
            value_acc[...] += nt(upstream, softened.astype(BF16))
            key_acc[...] += nt(queries, logit_grad)
            grads[0, member, :, at] = (nn(heads[1, member], logit_grad) * HD ** (-0.5)).astype(BF16)
            return carry

        steps = L // QB_BACK
        lax.fori_loop(0, steps, attend_back, 0)
        grads[1, member] = (key_acc[...] * LN2).astype(BF16)
        grads[2, member] = value_acc[...].astype(BF16)
        for copy in backward[member][0] + [backward[member][1]]:
            copy.start()
        if member == 0:
            near_sums(0)
            core_sums(1)
            core_sums(2)
        else:
            first_sums(0)
            near_sums(1)
            near_sums(2)
    loads["up"].wait()
    loads["mmid"].wait()
    loads["proj"].wait()
    loads["fdown"].wait()
    mixer_hat, mixer_inverse = norm_parts(mmid[...])
    mixer_normed = (mixer_hat * mgain_ref[...]).astype(BF16).T
    for copies, here in backward:
        for copy in copies:
            copy.wait_recv()
        here.wait()
    hold(0)
    first_sums(1)
    first_sums(2)
    packed_grad = back[...].reshape(3 * D, MB * ROWS)
    normed_grad = nn(proj[...], packed_grad).T
    residual, gain_rows = norm_pull(mixer_hat, mixer_inverse, mgain_ref[...], normed_grad)
    dmgain_ref[...] = jnp.sum(gain_rows, axis=0, keepdims=True)
    upstream = ups[...] + residual
    dproj[...] = nt(mixer_normed, packed_grad).astype(BF16)
    store(dproj, dproj_ref)
    grad = upstream.astype(BF16)
    normed_grad = jnp.zeros((MB * ROWS, D), F32)
    for part in range(2):
        cut = slice(part * FF // 2, (part + 1) * FF // 2)
        act, slope = gelu_parts(hidden[:, cut])
        hidden_grad = (slope * nt(grad, fdown[cut])).astype(BF16)
        normed_grad = normed_grad + nt(hidden_grad, fup[:, cut])
        ddown[cut] = tn(act.astype(BF16), grad).astype(BF16)
        dup[:, cut] = tn(first_normed, hidden_grad).astype(BF16)
    store(ddown, ddown_ref)
    store(dup, dup_ref)
    residual, gain_rows = norm_pull(first_hat, first_inverse, fgain_ref[...], normed_grad)
    dfgain_ref[...] = jnp.sum(gain_rows, axis=0, keepdims=True)
    upstream = upstream + residual
    lup[...] = upstream
    store(lup, lup_ref)
    grad = upstream.astype(BF16)
    loads["att"].wait()
    loads["ow"].wait()
    attended = att[...].reshape(MB * ROWS, D)
    attended_grad = nt(grad, ow[...]).astype(BF16)
    agrad[...] = attended_grad.reshape(MB, ROWS, D)
    store(agrad, agrad_ref)
    inner = jnp.sum(attended_grad.astype(F32) * attended, axis=1, keepdims=True)
    for member in range(MB):
        rows = slice(member * ROWS, (member + 1) * ROWS)
        spare = jnp.zeros((6, ROWS), F32)
        fig_ref[member] = jnp.concatenate(
            [clse_ref[member, 0:1], to_rows(inner[rows], inner[rows])[0:1], spare], axis=0
        )
    dout[...] = tn(attended.astype(BF16), grad).astype(BF16)
    store(dout, dout_ref)
    hold(1)
    hold(2)
    finish()
    for copy in stores:
        copy.wait()
    for copies, here in outward + backward:
        for copy in copies:
            copy.wait_send()


def latents_backward(collective_id, arrays, *args):
    dma = pltpu.SemaphoreType.DMA
    vmem = pl.BlockSpec(memory_space=pltpu.VMEM)
    hbm = pl.BlockSpec(memory_space=pl.ANY)
    rows = MB * ROWS
    sources, items, kinds, shapes = reduce_plan(arrays)
    reduced = [jax.ShapeDtypeStruct((rows_ // 2, columns), kind) for (rows_, columns), kind in zip(shapes, kinds)]
    stored = [
        ((MB, ROWS, D), BF16), ((MB, 8, ROWS), F32), ((rows, D), F32), ((D, FF), BF16), ((FF, D), BF16),
        ((D, 3 * D), BF16), ((D, D), BF16), ((1, D), F32), ((1, D), F32),
    ]
    return pl.pallas_call(
        functools.partial(latents_backward_kernel, items),
        in_specs=[hbm, hbm, hbm, vmem, hbm, hbm, hbm, hbm, vmem, hbm, vmem, hbm, hbm, vmem, hbm] + [hbm] * len(arrays),
        out_specs=[hbm, vmem] + [hbm] * 5 + [vmem] * (2 + len(arrays)),
        out_shape=[jax.ShapeDtypeStruct(shape, kind) for shape, kind in stored] + reduced,
        scratch_shapes=[
            pltpu.VMEM((3, MB, HD, L), BF16), pltpu.VMEM((MB, HD, L), F32), pltpu.VMEM((rows, D), F32),
            pltpu.VMEM((rows, D), F32), pltpu.VMEM((rows, D), F32), pltpu.VMEM((MB, ROWS, D), F32),
            pltpu.VMEM((D, D), BF16), pltpu.VMEM((D, FF), BF16), pltpu.VMEM((FF, D), BF16),
            pltpu.VMEM((D, 3 * D), BF16), pltpu.VMEM((L, HD), BF16), pltpu.VMEM((L, HD), BF16),
            pltpu.VMEM((1, MB, HD, L), BF16), pltpu.VMEM((HD, L), F32), pltpu.VMEM((HD, L), F32),
            pltpu.VMEM((3, MB, HD, L), BF16), pltpu.VMEM((3, H, HD, rows), BF16),
            pltpu.VMEM((MB, ROWS, D), BF16), pltpu.VMEM((rows, D), F32), pltpu.VMEM((D, FF), BF16),
            pltpu.VMEM((FF, D), BF16), pltpu.VMEM((D, 3 * D), BF16), pltpu.VMEM((D, D), BF16),
            pltpu.VMEM((rows, FF), F32),
            dma((10,)), dma((6,)), dma((7, MB)), dma((7, MB)), dma((MB,)), dma((7, MB)), dma((7, MB)), dma((MB,)),
        ] + tok_scratch(items, kinds),
        compiler_params=pltpu.CompilerParams(
            collective_id=collective_id, has_side_effects=True, vmem_limit_bytes=61 * MIB
        ),
        cost_estimate=pl.CostEstimate(
            flops=35 * 10**9, bytes_accessed=36 * 10**6, transcendentals=10 * 10**6
        ),
        name="latents_backward",
    )(*args, *sources)


def fast_body(
    tokens,
    latents,
    segments,
    scene_mask,
    counts,
    token_gain,
    query_gain,
    query_weight,
    key_weight,
    value_weight,
    output_weight,
    first_gain,
    first_up,
    first_down,
    mixer_gain,
    mixer_project,
    mixer_output,
    second_gain,
    second_up,
    second_down,
    cotangent,
):
    scenes = (segments, scene_mask, counts)
    keys, values, queries, attended, lse = cross_forward(
        0, tokens, latents, token_gain[None], query_gain[None], query_weight, key_weight, value_weight, *scenes
    )
    (latents_out, first_mid, mixer_mid, packed, exact, head_lse, upstream, mixed_grad, d_second_down, d_second_up,
     d_mixer_output, d_second_gain) = latents_forward(
        1, latents, attended, cotangent, output_weight, first_gain[None], first_up, first_down, mixer_gain[None],
        mixer_project, mixer_output, second_gain[None], second_up, second_down,
    )
    (attended_grad, figures, upstream, d_first_up, d_first_down, d_project, d_output, d_mixer_gain, d_first_gain,
     *early) = latents_backward(
        2, [d_second_up, d_second_down, d_mixer_output], mixed_grad, packed, exact, head_lse, upstream, mixer_mid,
        first_mid, attended, lse, output_weight, first_gain[None], first_up, first_down, mixer_gain[None], mixer_project,
    )
    latents_grad, tokens_grad, d_key, d_value, d_query, gains, *rest = cross_backward(
        5, early, [d_first_up, d_first_down, d_project], tokens, token_gain[None], key_weight, value_weight,
        *scenes, keys, values, queries, attended_grad, figures, latents, upstream, query_gain[None], query_weight,
        d_first_gain, d_mixer_gain, d_second_gain,
    )
    early, held = rest[:len(early)], rest[len(early):]
    o_output, o_key, o_value, o_query, gains, *late = reduce_grads(
        7, [d_output, d_key, d_value, d_query, gains], held, early
    )
    late, early = late[:len(held)], late[len(held):]
    (latents_out, latents_grad, tokens_grad, o_second_up, o_second_down, o_mixer_output, o_first_up, o_first_down,
     o_project, o_output, o_key, o_value, o_query, *o_gains) = write_results(
        [latents_out, latents_grad.reshape(latents_out.shape), tokens_grad, *early, *late, o_output, o_key, o_value, o_query], gains, 5
    )
    o_gains = [gain.reshape(D // TOK) for gain in o_gains]
    return (
        latents_out,
        latents_grad,
        tokens_grad,
        o_gains[0],
        o_gains[1],
        o_query,
        o_key,
        o_value,
        o_output,
        o_gains[2],
        o_first_up,
        o_first_down,
        o_gains[3],
        o_project,
        o_mixer_output,
        o_gains[4],
        o_second_up,
        o_second_down,
    )


IN_SPECS = (
    P("grp", None, "tok", None),
    P("grp", None, None, None),
    P("grp", None, "tok"),
    P("grp", None, None, None),
    P("grp", None, "tok"),
    P(),
    P(),
    P(),
    P(),
    P(),
    P(),
    P(),
    P(),
    P(),
    P(),
    P(),
    P(),
    P(),
    P(),
    P(),
    P("grp", None, "tok", None),
)
OUT_SPECS = (
    P("grp", None, "tok", None),
    P("grp", None, "tok", None),
    P("grp", None, "tok", None),
    P("tok"),
    P("tok"),
    P("tok", None),
    P("tok", None),
    P("tok", None),
    P("tok", None),
    P("tok"),
    P("tok", None),
    P("tok", None),
    P("tok"),
    P("tok", None),
    P("tok", None),
    P("tok"),
    P("tok", None),
    P("tok", None),
)


def solution(mesh):
    return jax.shard_map(
        fast_body if mesh.shape["tok"] == TOK else general_body,
        mesh=mesh,
        in_specs=IN_SPECS,
        out_specs=OUT_SPECS,
        check_vma=False,
    )
```

profile of v0, /device:TPU:0, one launch (start us, length us, event | category | flops | bytes accessed | tf_op | source)
XLA Modules:
  0.0 282.7 jit_solution(17202637449822400302)
XLA Ops:
  0.7 1.3 copy.39.count_ref
  2.0 41.2 %cross_forward.1 = (bf16[2,1024,512]{2,1,0:T(8,128)(2,1)}, bf16[2,1024,512]{2,1,0:T(8,128)(2,1)}, bf16[2,2048,512]{2,1,0:T(8,128)(2,1)}, f32[2,256,512]{2,1,0:T(8,128)}, f32[2,8,256]{2,1,0:T(8,128)}) custom-call(bf16[1,2,1024,512]{3,2,1,0:T(8,128)(2,1)} %tok_ref.3, f32[1,2,2048,512]{3,2,1,0:T(8,128)} %lat_ref.5, f32[1,512]{1,0:T(1,128)} %bitcast.33, ...), custom_call_target="tpu_custom_call" | custom-call | flops 14000000000 | bytes 22000000 | tf_op jit(solution)/shard_map/cross_forward/pallas_call | solution.py:667
  43.2 58.9 %latents_forward.1 = (f32[1,2,256,512]{3,2,1,0:T(8,128)}, f32[512,512]{1,0:T(8,128)}, f32[512,512]{1,0:T(8,128)}, bf16[3,2,64,2048]{3,2,1,0:T(8,128)(2,1)}, f32[...) custom-call(f32[1,2,2048,512]{3,2,1,0:T(8,128)} %lat_ref.5, ...), custom_call_target="tpu_custom_call" | custom-call | flops 20000000000 | bytes 30000000 | tf_op jit(solution)/shard_map/latents_forward/pallas_call | solution.py:1330
  102.1 63.8 %latents_backward.1 = (bf16[2,256,512]{2,1,0:T(8,128)(2,1)}, f32[2,8,256]{2,1,0:T(8,128)}, f32[512,512]{1,0:T(8,128)}, bf16[512,2048]{1,0:T(8,128)(2,1)}, bf16[2...) custom-call(bf16[1,8,64,512]{3,2,1,0:T(8,128)(2,1)} %get-tuple-eleme, ...), custom_call_target="tpu_custom_call" | custom-call | flops 35000000512 | bytes 36000000 | tf_op jit(solution)/shard_map/latents_backward/pallas_call | solution.py:1872
  165.9 66.2 %cross_backward.1 = (f32[512,512]{1,0:T(8,128)}, f32[1,2,1024,512]{3,2,1,0:T(8,128)}, bf16[512,512]{1,0:T(8,128)(2,1)}, bf16[512,512]{1,0:T(8,128)(2,1)}, bf16[5...) custom-call(bf16[1,2,1024,512]{3,2,1,0:T(8,128)(2,1)} %tok_ref.3, ...), custom_call_target="tpu_custom_call" | custom-call | flops 25999998976 | bytes 24000000 | tf_op jit(solution)/shard_map/cross_backward/pallas_call | solution.py:1123
  232.1 42.4 %reduce_grads.1 = (f32[64,512]{1,0:T(8,128)}, f32[64,512]{1,0:T(8,128)}, f32[64,512]{1,0:T(8,128)}, f32[64,512]{1,0:T(8,128)}, f32[16,128]{1,0:T(8,128)}, /*inde...) custom-call(bf16[2,2,2,64,512]{4,3,2,1,0:T(8,128)(2,1)} %bitcast.23,, ...), custom_call_target="tpu_custom_call" | custom-call | tf_op jit(solution)/shard_map/reduce_grads/pallas_call | solution.py:1662
  274.5 8.0 %write_results.1 = (f32[1,2,256,512]{3,2,1,0:T(8,128)}, f32[1,2,256,512]{3,2,1,0:T(8,128)}, f32[1,2,1024,512]{3,2,1,0:T(8,128)}, f32[64,2048]{1,0:T(8,128)}, f32...) custom-call(f32[1,2,256,512]{3,2,1,0:T(8,128)} %get-tuple-element.89, ...), custom_call_target="tpu_custom_call" | custom-call | tf_op jit(solution)/shard_map/write_results/pallas_call | solution.py:1697
where the time goes:
time: 285 us; the launch traced here: 283 us
  Pallas kernels  281 us (99%)
    pallas_call x1, Pallas kernels, cross_backward(): pl.pallas_call(functools.partial(cross_backward_kernel, items, grad_items...  66.2 us
    pallas_call x1, Pallas kernels, latents_backward(): pl.pallas_call(functools.partial(latents_backward_kernel, items), in_spec...  63.8 us
    pallas_call x1, Pallas kernels, latents_forward(): pl.pallas_call(latents_forward_kernel, in_specs=[hbm, hbm, hbm, hbm, vmem...  58.9 us
    pallas_call x1, Pallas kernels, reduce_grads(): pl.pallas_call(functools.partial(reduce_kernel, items, whole, joined, len...  42.4 us
    pallas_call x1, Pallas kernels, cross_forward(): pl.pallas_call(cross_forward_kernel, in_specs=[hbm, hbm] + [vmem] * 5 + [...  41.2 us
    pallas_call x1, Pallas kernels, write_results(): pl.pallas_call(functools.partial(write_kernel, n), in_specs=[hbm] * n + [...  8.03 us

commit v1 on v0

--- a/solution.py
+++ b/solution.py
@@ -857,8 +857,7 @@
     for flip in (1, 2):
         for copy in far_copies(flip):
             copy.start()
-    for item in range(more):
-        tok[0](item)
+    tok[0](0)
     for item in range(count):
         grp[0](item)
     for copy in masks:
@@ -964,10 +963,12 @@
                 for copy in far_copies(4 + flip):
                     copy.start()
             tok[1](0)
+            tok[0](1)
 
         @pl.when(step == 1)
         def _():
             pass_near(0)
+            tok[0](2)
 
         @pl.when(step == 2)
         def _():
@@ -997,20 +998,15 @@
                 copy.start()
             relay(0)
 
-        @pl.when(step == 4 * MB - 1)
+        return carry
+
+    lax.fori_loop(0, 4 * MB, step_body, 0)
+
+    def tokens_body(member, carry):
+        @pl.when(member == 1)
         def _():
             tok[3](0)
             tok[2](1)
-
-        return carry
-
-    lax.fori_loop(0, 4 * MB, step_body, 0)
-
-    def tokens_body(member, carry):
-        @pl.when(member == 1)
-        def _():
-            hold(0)
-            tok[2](2)
 
         for half in range(TOK_DEV // span):
             tokens_back(member, half)
@@ -1029,8 +1025,9 @@
     lax.fori_loop(0, MB, tokens_body, 0)
     dkw_ref[...] = dkw[...].astype(BF16)
     dvw_ref[...] = dvw[...].astype(BF16)
+    tok[2](2)
+    hold(0)
     tok[3](1)
-    tok[3](2)
     for copy in tails:
         copy.wait()
     gain = qgain_ref[...]
@@ -1047,6 +1044,7 @@
     dqw_ref[...] = tn(normed, asked_grad).astype(BF16)
     source_grad, gain_rows = norm_pull(hat, inverse, gain, nt(asked_grad, qw_ref[...]))
     lup[...] += source_grad
+    tok[3](2)
     last = pltpu.make_async_copy(lup, dlat_ref, tail_sem.at[2])
     last.start()
     query_gain = jnp.sum(gain_rows, axis=0, keepdims=True)
@@ -1197,7 +1195,7 @@
     dgain_ref,
     lat, att, cot, ow, fup, fdown, proj, mow, sup, sdown,
     out, fmid, mmid, heads, exact, up, mgrad, ddown, dup, dmo,
-    rows_out, keys, values, mixed, mixed_rows,
+    rows_out, keys, values, mixed, mixed_rows, active, hidden_low, normed_low,
     load_sem, store_sem, send_a, recv_a, local_a, send_b, recv_b, local_b,
 ):
     me, peers = all_peers()
@@ -1220,31 +1218,35 @@
     flat = (MB * ROWS, D)
     for name in ("lat", "att", "ow"):
         loads[name].wait()
-    first = lat[...].reshape(flat) + nn(att[...].reshape(flat).astype(BF16), ow[...])
-    fmid[...] = first
-    store(fmid, fmid_ref)
-    normed = (norm_parts(first)[0] * fgain_ref[...]).astype(BF16)
-    loads["fup"].wait()
-    loads["fdown"].wait()
-    mid = first
-    for part in range(2):
-        cut = slice(part * FF // 2, (part + 1) * FF // 2)
-        mid = mid + nn(jax.nn.gelu(nn(normed, fup[:, cut])).astype(BF16), fdown[cut])
-    mmid[...] = mid
-    store(mmid, mmid_ref)
-    normed = (norm_parts(mid)[0] * mgain_ref[...]).astype(BF16).T
-    loads["proj"].wait()
-    for kind, scale in enumerate((HD ** (-0.5) * LOG2E, 1.0, 1.0)):
-        packed = tn(proj[:, kind * D:(kind + 1) * D], normed) * scale
-        rows_out[kind] = packed.astype(BF16).reshape(H, HD, MB * ROWS)
     outward = [head_copies(rows_out, heads, True, member, me, peers, send_a, recv_a, local_a) for member in range(MB)]
     backward = [
         head_copies(mixed_rows, mixed, False, member, me, peers, send_b, recv_b, local_b) for member in range(MB)
     ]
-    for copies, here in outward:
+    for member in range(MB):
+        rows = slice(member * ROWS, (member + 1) * ROWS)
+        first = lat[member] + nn(att[member].astype(BF16), ow[...])
+        fmid[rows] = first
+        normed = (norm_parts(first)[0] * fgain_ref[...]).astype(BF16)
+        if member == 0:
+            loads["fup"].wait()
+            loads["fdown"].wait()
+        mid = first
+        for part in range(2):
+            cut = slice(part * FF // 2, (part + 1) * FF // 2)
+            mid = mid + nn(jax.nn.gelu(nn(normed, fup[:, cut])).astype(BF16), fdown[cut])
+        mmid[rows] = mid
+        normed = (norm_parts(mid)[0] * mgain_ref[...]).astype(BF16).T
+        if member == 0:
+            loads["proj"].wait()
+        for kind, scale in enumerate((HD ** (-0.5) * LOG2E, 1.0, 1.0)):
+            packed = tn(proj[:, kind * D:(kind + 1) * D], normed) * scale
+            rows_out[kind, :, :, rows] = packed.astype(BF16).reshape(H, HD, ROWS)
+        copies, here = outward[member]
         for copy in copies:
             copy.start()
         here.start()
+    store(fmid, fmid_ref)
+    store(mmid, mmid_ref)
     for member in range(MB):
         copies, here = outward[member]
         for copy in copies:
@@ -1275,40 +1277,45 @@
     loads["sup"].wait()
     loads["sdown"].wait()
     loads["cot"].wait()
-    for copies, here in backward:
+    gains = []
+    for member in range(MB):
+        copies, here = backward[member]
         for copy in copies:
             copy.wait_recv()
         here.wait()
-    mixed_t = mixed_rows[0].reshape(D, MB * ROWS)
-    second = mmid[...] + tn(mixed_t, mow[...])
-    hat, inverse = norm_parts(second)
-    normed = (hat * sgain_ref[...]).astype(BF16)
-    upstream = cot[...].reshape(flat)
-    grad = upstream.astype(BF16)
-    final = second
-    normed_grad = jnp.zeros(flat, F32)
-    for part in range(2):
-        cut = slice(part * FF // 2, (part + 1) * FF // 2)
-        act, slope = gelu_parts(nn(normed, sup[:, cut]))
-        act = act.astype(BF16)
-        final = final + nn(act, sdown[cut])
-        hidden_grad = (slope * nt(grad, sdown[cut])).astype(BF16)
-        normed_grad = normed_grad + nt(hidden_grad, sup[:, cut])
-        ddown[cut] = tn(act, grad).astype(BF16)
-        dup[:, cut] = tn(normed, hidden_grad).astype(BF16)
+        rows = slice(member * ROWS, (member + 1) * ROWS)
+        second = mmid[rows] + tn(mixed_rows[0, :, :, rows].reshape(D, ROWS), mow[...])
+        hat, inverse = norm_parts(second)
+        normed = (hat * sgain_ref[...]).astype(BF16)
+        normed_low[rows] = normed
+        upstream = cot[member]
+        grad = upstream.astype(BF16)
+        final = second
+        normed_grad = jnp.zeros((ROWS, D), F32)
+        for part in range(2):
+            cut = slice(part * FF // 2, (part + 1) * FF // 2)
+            act, slope = gelu_parts(nn(normed, sup[:, cut]))
+            act = act.astype(BF16)
+            active[rows, cut] = act
+            final = final + nn(act, sdown[cut])
+            hidden_grad = (slope * nt(grad, sdown[cut])).astype(BF16)
+            hidden_low[rows, cut] = hidden_grad
+            normed_grad = normed_grad + nt(hidden_grad, sup[:, cut])
+        out[member] = final
+        residual, gain_rows = norm_pull(hat, inverse, sgain_ref[...], normed_grad)
+        gains.append(jnp.sum(gain_rows, axis=0, keepdims=True))
+        upstream = upstream + residual
+        up[rows] = upstream
+        mgrad[0, :, :, rows] = nt(mow[...], upstream.astype(BF16)).astype(BF16).reshape(H, HD, ROWS)
+    store(out, out_ref.at[0])
+    store(up, up_ref)
+    store(mgrad, mgrad_ref)
+    dgain_ref[...] = gains[0] + gains[1]
+    ddown[...] = tn(active[...], cot[...].reshape(flat).astype(BF16)).astype(BF16)
     store(ddown, ddown_ref)
+    dup[...] = tn(normed_low[...], hidden_low[...]).astype(BF16)
     store(dup, dup_ref)
-    out[...] = final.reshape(MB, ROWS, D)
-    store(out, out_ref.at[0])
-    residual, gain_rows = norm_pull(hat, inverse, sgain_ref[...], normed_grad)
-    dgain_ref[...] = jnp.sum(gain_rows, axis=0, keepdims=True)
-    upstream = upstream + residual
-    up[...] = upstream
-    store(up, up_ref)
-    grad = upstream.astype(BF16)
-    mgrad[0] = nt(mow[...], grad).astype(BF16).reshape(H, HD, MB * ROWS)
-    store(mgrad, mgrad_ref)
-    dmo[...] = nn(mixed_t, grad).astype(BF16)
+    dmo[...] = nn(mixed_rows[0].reshape(D, MB * ROWS), up[...].astype(BF16)).astype(BF16)
     store(dmo, dmo_ref)
     for copy in stores:
         copy.wait()
@@ -1343,6 +1350,7 @@
             pltpu.VMEM((D, D), BF16),
             pltpu.VMEM((3, H, HD, rows), BF16), pltpu.VMEM((L, HD), BF16), pltpu.VMEM((HD + 16, L), BF16),
             pltpu.VMEM((1, MB, HD, L), BF16), pltpu.VMEM((1, H, HD, rows), BF16),
+            pltpu.VMEM((rows, FF), BF16), pltpu.VMEM((rows, FF), BF16), pltpu.VMEM((rows, D), BF16),
             dma((10,)), dma((11,)), dma((7, MB)), dma((7, MB)), dma((MB,)), dma((7, MB)), dma((7, MB)), dma((MB,)),
         ],
         compiler_params=pltpu.CompilerParams(
@@ -1565,7 +1573,7 @@
 
 
 def add(target, one, two):
-    target[...] = (one[...].astype(F32) + two[...].astype(F32)).astype(target.dtype)
+    target[...] = one[...] + two[...]
 
 
 def reduce_kernel(items, whole, joined, count, *refs):
@@ -1594,12 +1602,12 @@
         first[5](i)
     for i in range(n):
         tok[2](i)
-    early[1](0)
     for i in range(n):
         tok[3](i)
     for i in range(n):
         own_held[i][...] = tok[4](i).astype(own_held[i].dtype)
         late[0](i)
+    early[1](0)
     for i in range(1, m):
         early[1](i)
         early[2](i - 1)
@@ -1717,10 +1725,10 @@
     reduced = refs[24 + count:24 + 2 * count]
     rest = refs[24 + 2 * count:]
     (heads, exact, ups, mmid, fmid, att, ow, fup, fdown, proj, keys, values, upstream_heads, key_acc, value_acc,
-     grads, back, agrad, lup, dup, ddown, dproj, dout, hidden,
-     load_sem, store_sem, send_a, recv_a, local_a, send_b, recv_b, local_b) = rest[:32]
+     grads, back, agrad, lup, dup, ddown, dproj, dout, hidden, active, hidden_low, grad_low,
+     load_sem, store_sem, send_a, recv_a, local_a, send_b, recv_b, local_b) = rest[:35]
     me, peers = all_peers()
-    reducer, near_devices = tok_steps(items, sources, rest[32:])
+    reducer, near_devices = tok_steps(items, sources, rest[35:])
     core_sends, core_sums, near_sums, first_sums, second_sums, finish = reducer
     odd, level_near, level_far = levels()
 
@@ -1750,8 +1758,7 @@
         for copy in copies:
             copy.start()
         here.start()
-    for item in range(3):
-        core_sends(item)
+    core_sends(0)
     loads["fmid"].wait()
     loads["fup"].wait()
     first_hat, first_inverse = norm_parts(fmid[...])
@@ -1769,6 +1776,9 @@
         for copy in copies:
             copy.wait_recv()
         here.wait()
+        if member == 0:
+            core_sends(1)
+            core_sends(2)
 
         def attend_back(step, carry, member=member):
             at = pl.ds(pl.multiple_of(step * QB_BACK, QB_BACK), QB_BACK)
@@ -1802,51 +1812,58 @@
     loads["fdown"].wait()
     mixer_hat, mixer_inverse = norm_parts(mmid[...])
     mixer_normed = (mixer_hat * mgain_ref[...]).astype(BF16).T
-    for copies, here in backward:
+    loads["att"].wait()
+    loads["ow"].wait()
+    mixer_gains, first_gains = [], []
+
+    def rows_back(member):
+        copies, here = backward[member]
         for copy in copies:
             copy.wait_recv()
         here.wait()
+        rows = slice(member * ROWS, (member + 1) * ROWS)
+        normed_grad = nn(proj[...], back[:, :, :, rows].reshape(3 * D, ROWS)).T
+        residual, gain_rows = norm_pull(mixer_hat[rows], mixer_inverse[rows], mgain_ref[...], normed_grad)
+        mixer_gains.append(jnp.sum(gain_rows, axis=0, keepdims=True))
+        upstream = ups[rows] + residual
+        grad = upstream.astype(BF16)
+        grad_low[rows] = grad
+        normed_grad = jnp.zeros((ROWS, D), F32)
+        for part in range(2):
+            cut = slice(part * FF // 2, (part + 1) * FF // 2)
+            act, slope = gelu_parts(hidden[rows, cut])
+            active[rows, cut] = act.astype(BF16)
+            hidden_grad = (slope * nt(grad, fdown[cut])).astype(BF16)
+            hidden_low[rows, cut] = hidden_grad
+            normed_grad = normed_grad + nt(hidden_grad, fup[:, cut])
+        residual, gain_rows = norm_pull(first_hat[rows], first_inverse[rows], fgain_ref[...], normed_grad)
+        first_gains.append(jnp.sum(gain_rows, axis=0, keepdims=True))
+        upstream = upstream + residual
+        lup[rows] = upstream
+        attended_grad = nt(upstream.astype(BF16), ow[...]).astype(BF16)
+        agrad[member] = attended_grad
+        inner = jnp.sum(attended_grad.astype(F32) * att[member], axis=1, keepdims=True)
+        fig_ref[member] = jnp.concatenate(
+            [clse_ref[member, 0:1], to_rows(inner, inner)[0:1], jnp.zeros((6, ROWS), F32)], axis=0
+        )
+
+    rows_back(0)
     hold(0)
     first_sums(1)
     first_sums(2)
-    packed_grad = back[...].reshape(3 * D, MB * ROWS)
-    normed_grad = nn(proj[...], packed_grad).T
-    residual, gain_rows = norm_pull(mixer_hat, mixer_inverse, mgain_ref[...], normed_grad)
-    dmgain_ref[...] = jnp.sum(gain_rows, axis=0, keepdims=True)
-    upstream = ups[...] + residual
-    dproj[...] = nt(mixer_normed, packed_grad).astype(BF16)
+    rows_back(1)
+    store(lup, lup_ref)
+    store(agrad, agrad_ref)
+    dmgain_ref[...] = mixer_gains[0] + mixer_gains[1]
+    dfgain_ref[...] = first_gains[0] + first_gains[1]
+    grad = grad_low[...]
+    ddown[...] = tn(active[...], grad).astype(BF16)
+    store(ddown, ddown_ref)
+    dup[...] = tn(first_normed, hidden_low[...]).astype(BF16)
+    store(dup, dup_ref)
+    dproj[...] = nt(mixer_normed, back[...].reshape(3 * D, MB * ROWS)).astype(BF16)
     store(dproj, dproj_ref)
-    grad = upstream.astype(BF16)
-    normed_grad = jnp.zeros((MB * ROWS, D), F32)
-    for part in range(2):
-        cut = slice(part * FF // 2, (part + 1) * FF // 2)
-        act, slope = gelu_parts(hidden[:, cut])
-        hidden_grad = (slope * nt(grad, fdown[cut])).astype(BF16)
-        normed_grad = normed_grad + nt(hidden_grad, fup[:, cut])
-        ddown[cut] = tn(act.astype(BF16), grad).astype(BF16)
-        dup[:, cut] = tn(first_normed, hidden_grad).astype(BF16)
-    store(ddown, ddown_ref)
-    store(dup, dup_ref)
-    residual, gain_rows = norm_pull(first_hat, first_inverse, fgain_ref[...], normed_grad)
-    dfgain_ref[...] = jnp.sum(gain_rows, axis=0, keepdims=True)
-    upstream = upstream + residual
-    lup[...] = upstream
-    store(lup, lup_ref)
-    grad = upstream.astype(BF16)
-    loads["att"].wait()
-    loads["ow"].wait()
-    attended = att[...].reshape(MB * ROWS, D)
-    attended_grad = nt(grad, ow[...]).astype(BF16)
-    agrad[...] = attended_grad.reshape(MB, ROWS, D)
-    store(agrad, agrad_ref)
-    inner = jnp.sum(attended_grad.astype(F32) * attended, axis=1, keepdims=True)
-    for member in range(MB):
-        rows = slice(member * ROWS, (member + 1) * ROWS)
-        spare = jnp.zeros((6, ROWS), F32)
-        fig_ref[member] = jnp.concatenate(
-            [clse_ref[member, 0:1], to_rows(inner[rows], inner[rows])[0:1], spare], axis=0
-        )
-    dout[...] = tn(attended.astype(BF16), grad).astype(BF16)
+    dout[...] = tn(att[...].reshape(MB * ROWS, D).astype(BF16), lup[...].astype(BF16)).astype(BF16)
     store(dout, dout_ref)
     hold(1)
     hold(2)
@@ -1883,7 +1900,8 @@
             pltpu.VMEM((3, MB, HD, L), BF16), pltpu.VMEM((3, H, HD, rows), BF16),
             pltpu.VMEM((MB, ROWS, D), BF16), pltpu.VMEM((rows, D), F32), pltpu.VMEM((D, FF), BF16),
             pltpu.VMEM((FF, D), BF16), pltpu.VMEM((D, 3 * D), BF16), pltpu.VMEM((D, D), BF16),
-            pltpu.VMEM((rows, FF), F32),
+            pltpu.VMEM((rows, FF), F32), pltpu.VMEM((rows, FF), BF16), pltpu.VMEM((rows, FF), BF16),
+            pltpu.VMEM((rows, D), BF16),
             dma((10,)), dma((6,)), dma((7, MB)), dma((7, MB)), dma((MB,)), dma((7, MB)), dma((7, MB)), dma((MB,)),
         ] + tok_scratch(items, kinds),
         compiler_params=pltpu.CompilerParams(

time: 285 us -> 280 us (0.982)
  Pallas kernels: 281 us -> 275 us
    pallas_call x1, Pallas kernels: 58.9 us -> 54.2 us  [latents_forward(): pl.pallas_call(latents_forward_kernel, in_specs=[hbm, hbm, hbm, hbm, vmem...]
where the time goes in v1:
time: 280 us; the launch traced here: 277 us
  Pallas kernels  275 us (98%)
    pallas_call x1, Pallas kernels, cross_backward(): pl.pallas_call(functools.partial(cross_backward_kernel, items, grad_items...  66.9 us
    pallas_call x1, Pallas kernels, latents_backward(): pl.pallas_call(functools.partial(latents_backward_kernel, items), in_spec...  61.2 us
    pallas_call x1, Pallas kernels, latents_forward(): pl.pallas_call(latents_forward_kernel, in_specs=[hbm, hbm, hbm, hbm, vmem...  54.2 us
    pallas_call x1, Pallas kernels, reduce_grads(): pl.pallas_call(functools.partial(reduce_kernel, items, whole, joined, len...  43.3 us
    pallas_call x1, Pallas kernels, cross_forward(): pl.pallas_call(cross_forward_kernel, in_specs=[hbm, hbm] + [vmem] * 5 + [...  41.2 us
    pallas_call x1, Pallas kernels, write_results(): pl.pallas_call(functools.partial(write_kernel, n), in_specs=[hbm] * n + [...  8.03 us

profile of v1, /device:TPU:0, one launch (start us, length us, event | category | flops | bytes accessed | tf_op | source)
XLA Modules:
  0.0 277.0 jit_solution(16592011041489157154)
XLA Ops:
  0.7 1.3 copy.39.count_ref
  2.0 41.2 %cross_forward.1 = (bf16[2,1024,512]{2,1,0:T(8,128)(2,1)}, bf16[2,1024,512]{2,1,0:T(8,128)(2,1)}, bf16[2,2048,512]{2,1,0:T(8,128)(2,1)}, f32[2,256,512]{2,1,0:T(8,128)}, f32[2,8,256]{2,1,0:T(8,128)}) custom-call(bf16[1,2,1024,512]{3,2,1,0:T(8,128)(2,1)} %tok_ref.3, f32[1,2,2048,512]{3,2,1,0:T(8,128)} %lat_ref.5, f32[1,512]{1,0:T(1,128)} %bitcast.33, ...), custom_call_target="tpu_custom_call" | custom-call | flops 14000000000 | bytes 22000000 | tf_op jit(solution)/shard_map/cross_forward/pallas_call | solution.py:667
  43.2 54.2 %latents_forward.1 = (f32[1,2,256,512]{3,2,1,0:T(8,128)}, f32[512,512]{1,0:T(8,128)}, f32[512,512]{1,0:T(8,128)}, bf16[3,2,64,2048]{3,2,1,0:T(8,128)(2,1)}, f32[...) custom-call(f32[1,2,2048,512]{3,2,1,0:T(8,128)} %lat_ref.5, ...), custom_call_target="tpu_custom_call" | custom-call | flops 20000000000 | bytes 30000000 | tf_op jit(solution)/shard_map/latents_forward/pallas_call | solution.py:1337
  97.4 61.2 %latents_backward.1 = (bf16[2,256,512]{2,1,0:T(8,128)(2,1)}, f32[2,8,256]{2,1,0:T(8,128)}, f32[512,512]{1,0:T(8,128)}, bf16[512,2048]{1,0:T(8,128)(2,1)}, bf16[2...) custom-call(bf16[1,8,64,512]{3,2,1,0:T(8,128)(2,1)} %get-tuple-eleme, ...), custom_call_target="tpu_custom_call" | custom-call | flops 35000000512 | bytes 36000000 | tf_op jit(solution)/shard_map/latents_backward/pallas_call | solution.py:1889
  158.6 66.9 %cross_backward.1 = (f32[512,512]{1,0:T(8,128)}, f32[1,2,1024,512]{3,2,1,0:T(8,128)}, bf16[512,512]{1,0:T(8,128)(2,1)}, bf16[512,512]{1,0:T(8,128)(2,1)}, bf16[5...) custom-call(bf16[1,2,1024,512]{3,2,1,0:T(8,128)(2,1)} %tok_ref.3, ...), custom_call_target="tpu_custom_call" | custom-call | flops 25999998976 | bytes 24000000 | tf_op jit(solution)/shard_map/cross_backward/pallas_call | solution.py:1121
  225.5 43.3 %reduce_grads.1 = (f32[64,512]{1,0:T(8,128)}, f32[64,512]{1,0:T(8,128)}, f32[64,512]{1,0:T(8,128)}, f32[64,512]{1,0:T(8,128)}, f32[16,128]{1,0:T(8,128)}, /*inde...) custom-call(bf16[2,2,2,64,512]{4,3,2,1,0:T(8,128)(2,1)} %bitcast.23,, ...), custom_call_target="tpu_custom_call" | custom-call | tf_op jit(solution)/shard_map/reduce_grads/pallas_call | solution.py:1670
  268.8 8.0 %write_results.1 = (f32[1,2,256,512]{3,2,1,0:T(8,128)}, f32[1,2,256,512]{3,2,1,0:T(8,128)}, f32[1,2,1024,512]{3,2,1,0:T(8,128)}, f32[64,2048]{1,0:T(8,128)}, f32...) custom-call(f32[1,2,256,512]{3,2,1,0:T(8,128)} %get-tuple-element.89, ...), custom_call_target="tpu_custom_call" | custom-call | tf_op jit(solution)/shard_map/write_results/pallas_call | solution.py:1705

commit v2 on v1

--- a/solution.py
+++ b/solution.py
@@ -907,6 +907,7 @@
             weights.append(weight.astype(BF16))
         weight = jnp.concatenate(weights, axis=0)
         grad = jnp.concatenate(grads, axis=0)
+        middle(step)
         dv[member] += tn(weight, upstream)
         dk[member] += tn(grad, asked)
         asked_grad = (nn(grad, keys[member]) * D ** (-0.5)).astype(BF16)
@@ -950,12 +951,33 @@
     def hold(item):
         helds[item][...] = tok[4](item).astype(helds[item].dtype)
 
+    def middle(step):
+        @pl.when(step > 0)
+        def _():
+            combine(step - 1)
+
+        @pl.when(step == 1)
+        def _():
+            pass_near(0)
+
+        @pl.when(step == 3)
+        def _():
+            pass_on(3)
+            pass_near(1)
+
+        @pl.when(step == 5)
+        def _():
+            for copy in half_copies(0):
+                copy.start()
+
+        @pl.when(step == 6)
+        def _():
+            for copy in half_copies(1):
+                copy.start()
+            relay(0)
+
     def step_body(step, carry):
         compute(step)
-
-        @pl.when(step > 0)
-        def _():
-            combine(step - 1)
 
         @pl.when(step == 0)
         def _():
@@ -967,55 +989,41 @@
 
         @pl.when(step == 1)
         def _():
-            pass_near(0)
             tok[0](2)
 
         @pl.when(step == 2)
         def _():
             tok[1](1)
-
-        @pl.when(step == 3)
-        def _():
-            pass_on(3)
-            pass_near(1)
 
         @pl.when(step == 4)
         def _():
             pass_on(7)
             for item in range(count):
                 grp[4](item)
+            tok[2](0)
             tok[1](2)
 
-        @pl.when(step == 5)
-        def _():
-            for copy in half_copies(0):
-                copy.start()
-            tok[2](0)
-
         @pl.when(step == 6)
         def _():
-            for copy in half_copies(1):
-                copy.start()
-            relay(0)
+            tok[3](0)
+
+        @pl.when(step == 4 * MB - 1)
+        def _():
+            combine(step)
+            relay(1)
 
         return carry
 
     lax.fori_loop(0, 4 * MB, step_body, 0)
 
     def tokens_body(member, carry):
-        @pl.when(member == 1)
-        def _():
-            tok[3](0)
-            tok[2](1)
-
         for half in range(TOK_DEV // span):
             tokens_back(member, half)
         out_copy(member).start()
 
         @pl.when(member == 0)
         def _():
-            combine(4 * MB - 1)
-            relay(1)
+            helds[1][...] = tok[6](1)
 
         return carry
 
@@ -1025,9 +1033,8 @@
     lax.fori_loop(0, MB, tokens_body, 0)
     dkw_ref[...] = dkw[...].astype(BF16)
     dvw_ref[...] = dvw[...].astype(BF16)
-    tok[2](2)
     hold(0)
-    tok[3](1)
+    helds[2][...] = tok[6](2)
     for copy in tails:
         copy.wait()
     gain = qgain_ref[...]
@@ -1044,7 +1051,6 @@
     dqw_ref[...] = tn(normed, asked_grad).astype(BF16)
     source_grad, gain_rows = norm_pull(hat, inverse, gain, nt(asked_grad, qw_ref[...]))
     lup[...] += source_grad
-    tok[3](2)
     last = pltpu.make_async_copy(lup, dlat_ref, tail_sem.at[2])
     last.start()
     query_gain = jnp.sum(gain_rows, axis=0, keepdims=True)
@@ -1056,9 +1062,7 @@
     for device in range(TOK):
         gains_ref[16 * device:16 * device + 8, 0:width] = rows[:, device * width:(device + 1) * width]
     grp[3]((0,))
-    hold(1)
-    hold(2)
-    tok[5]()
+    tok[5]((1, 2))
     last.wait()
     for step in range(4, 4 * MB):
         core_copy(jnp.int32(step)).wait_send()
@@ -1130,7 +1134,10 @@
             jax.ShapeDtypeStruct((D, D), BF16),
             jax.ShapeDtypeStruct((16 * TOK, 128), F32),
         ] + [jax.ShapeDtypeStruct(array.shape, array.dtype) for array in arrays]
-        + [jax.ShapeDtypeStruct((high // 2, wide), kind) for (high, wide), kind in zip(shapes, grad_kinds)],
+        + [
+            jax.ShapeDtypeStruct((() if i == 0 else (2, 2)) + (high // 2, wide), kind)
+            for i, ((high, wide), kind) in enumerate(zip(shapes, grad_kinds))
+        ],
         scratch_shapes=scratch + grp_scratch(items, kinds) + tok_scratch(grad_items, grad_kinds),
         compiler_params=pltpu.CompilerParams(
             collective_id=collective_id, has_side_effects=True, vmem_limit_bytes=60 * MIB
@@ -1443,14 +1450,60 @@
         second_copy(i).wait_recv()
         return mine[i][y, x, keep].astype(F32) + second_in[i][...].astype(F32)
 
+    def near_hold(i):
+        keep, away = half_slices(items[i][1], odd)
+        near_copy(i).wait_recv()
+        return mine[i][:, :, keep] + near_in[i][...]
+
+    def finish(near_only=()):
+        for i in range(n):
+            core_copies(i)[0].wait_send()
+            near_copy(i).wait_send()
+            if i not in near_only:
+                for copy in (first_copy(i), second_copy(i)):
+                    copy.wait_send()
+
+    return (core_sends, core_sums, near_sums, first_sums, second_sums, finish, near_hold), (
+        mate, 2 * flip_x + core, 2 * flip_y + core)
+
+
+def quad_steps(items, quads, results, scratch):
+    n = len(items)
+    first_in, joined, second_in = [scratch[i * n:(i + 1) * n] for i in range(3)]
+    one_send, one_recv, two_send, two_recv = scratch[3 * n:]
+    me, core, chip, mate, (far, flip_x, flip_y) = places()
+    x, y = lax.rem(chip, 2), lax.div(chip, 2)
+
+    def first_copy(i):
+        x_first = items[i][-1]
+        source = quads[i].at[:, 1 - x] if x_first else quads[i].at[1 - y]
+        peer = 2 * (flip_x if x_first else flip_y) + core
+        return remote(source, first_in[i], one_send.at[i], one_recv.at[i], peer)
+
+    def second_copy(i):
+        x_first = items[i][-1]
+        source = joined[i].at[1 - y] if x_first else joined[i].at[1 - x]
+        peer = 2 * (flip_y if x_first else flip_x) + core
+        return remote(source, second_in[i], two_send.at[i], two_recv.at[i], peer)
+
+    def first_start(i):
+        first_copy(i).start()
+
+    def first_sums(i):
+        first_copy(i).wait_recv()
+        add(joined[i], quads[i].at[:, x] if items[i][-1] else quads[i].at[y], first_in[i])
+        second_copy(i).start()
+
+    def second_sums(i):
+        second_copy(i).wait_recv()
+        add(results[i], joined[i].at[y] if items[i][-1] else joined[i].at[x], second_in[i])
+
     def finish():
         for i in range(n):
-            core_copies(i)[0].wait_send()
-            for copy in (near_copy(i), first_copy(i), second_copy(i)):
+            for copy in (first_copy(i), second_copy(i)):
                 copy.wait_send()
 
-    return (core_sends, core_sums, near_sums, first_sums, second_sums, finish), (
-        mate, 2 * flip_x + core, 2 * flip_y + core)
+    return first_start, first_sums, second_sums, finish
 
 
 def plain_steps(items, sources, scratch):
@@ -1576,51 +1629,66 @@
     target[...] = one[...] + two[...]
 
 
-def reduce_kernel(items, whole, joined, count, *refs):
-    n, m, k = len(items), len(whole), len(joined)
-    sources, held, done = refs[:count], refs[count:count + m], refs[count + m:count + m + k]
-    refs = refs[count + m + k:]
-    outs, whole_outs, joined_outs = refs[:count], refs[count:count + m], refs[count + m:count + m + k]
-    scratch = refs[count + m + k:]
-    cut = 5 * n + 9
-    own_held = scratch[cut:cut + n]
-    tok, near_devices = plain_steps(items, sources, scratch[:cut])
-    cut += n
-    late, grp_devices = grp_steps(items, own_held, outs, scratch[cut:cut + 3 * n + 2])
-    cut += 3 * n + 2
-    early, unused = grp_steps(whole, held, whole_outs, scratch[cut:cut + 3 * m + 2])
-    cut += 3 * m + 2
-    first, unused = grp_steps(joined, done, joined_outs, scratch[cut:], done)
+def reduce_kernel(items, whole, square, joined, count, *refs):
+    n, m, q, k = len(items), len(whole), len(square), len(joined)
+
+    def take(length):
+        nonlocal refs
+        head, refs = refs[:length], refs[length:]
+        return head
+
+    sources, held, quads, done = take(count), take(m), take(q), take(k)
+    outs, whole_outs, quad_outs, joined_outs = take(count), take(m), take(q), take(k)
+    tok, near_devices = plain_steps(items, sources, take(5 * n + 9))
+    own_held = take(n)
+    late, grp_devices = grp_steps(items, own_held, outs, take(3 * n + 2))
+    early, unused = grp_steps(whole, held, whole_outs, take(3 * m + 2))
+    quad_held = take(q)
+    sums = quad_steps(square, quads, quad_held, take(3 * q + 4))
+    mid, unused = grp_steps(square, quad_held, quad_outs, take(3 * q + 2))
+    first, unused = grp_steps(joined, done, joined_outs, refs, done)
     greet_all(near_devices, grp_devices)
     for i in range(n):
         tok[0](i)
     for i in range(m):
         early[0](i)
+    for i in range(q):
+        sums[0](i)
     for i in range(n):
         tok[1](i)
     for i in range(k):
         first[5](i)
+    for i in range(q):
+        sums[1](i)
     for i in range(n):
         tok[2](i)
+    for i in range(q):
+        sums[2](i)
+        mid[0](i)
     for i in range(n):
         tok[3](i)
     for i in range(n):
         own_held[i][...] = tok[4](i).astype(own_held[i].dtype)
         late[0](i)
-    early[1](0)
-    for i in range(1, m):
+    for i in range(m):
         early[1](i)
-        early[2](i - 1)
     for i in range(k):
         first[2](i)
+    for i in range(q):
+        mid[1](i)
     for i in range(n):
         late[1](i)
-    early[2](m - 1)
+    for i in range(m):
+        early[2](i)
+    for i in range(q):
+        mid[2](i)
     for i in range(n):
         late[2](i)
     tok[-1]()
+    sums[-1]()
     late[3]()
     early[3]()
+    mid[3]()
     first[3]((1,))
 
 
@@ -1644,6 +1712,18 @@
     return [pltpu.VMEM(lead + (item[1] // part, item[3]), kind) for item, kind in zip(items, kinds)]
 
 
+def quad_plan(arrays, x_firsts):
+    items = tuple(
+        (i, 2 * array.shape[2], 0, array.shape[3], 0, x_first) for i, (array, x_first) in enumerate(zip(arrays, x_firsts))
+    )
+    return items, [array.dtype for array in arrays]
+
+
+def quad_scratch(items, kinds):
+    blocks = functools.partial(item_blocks, items, kinds)
+    return blocks((2,), 2) + blocks((2,), 2) + blocks((), 2) + [pltpu.SemaphoreType.DMA((len(items),))] * 4
+
+
 def plain_scratch(items, kinds):
     blocks = functools.partial(item_blocks, items, kinds)
     return (blocks((2, 2), 1) + blocks((2, 2), 1) + blocks((), 2) + blocks((2,), 1) + blocks((), 1)
@@ -1661,25 +1741,28 @@
     return blocks((), 2) * 3 + [pltpu.SemaphoreType.DMA((len(items), 2))] * 2
 
 
-def reduce_grads(collective_id, arrays, held, done):
+def reduce_grads(collective_id, arrays, held, quads, x_firsts, done):
     sources, items, kinds, shapes = reduce_plan(arrays)
     whole, whole_kinds = held_plan(held)
+    square, square_kinds = quad_plan(quads, x_firsts)
     joined, joined_kinds = held_plan(done)
     vmem = pl.BlockSpec(memory_space=pltpu.VMEM)
     hbm = pl.BlockSpec(memory_space=pl.ANY)
+    rest = len(held) + len(quads) + len(done)
     return pl.pallas_call(
-        functools.partial(reduce_kernel, items, whole, joined, len(arrays)),
-        in_specs=[hbm] * len(arrays) + [vmem] * (len(held) + len(done)),
-        out_specs=[vmem] * (len(arrays) + len(held) + len(done)),
+        functools.partial(reduce_kernel, items, whole, square, joined, len(arrays)),
+        in_specs=[hbm] * len(arrays) + [vmem] * rest,
+        out_specs=[vmem] * (len(arrays) + rest),
         out_shape=[jax.ShapeDtypeStruct(shape, F32) for shape in shapes]
-        + [jax.ShapeDtypeStruct((item[1], item[3]), F32) for item in whole + joined],
+        + [jax.ShapeDtypeStruct((item[1], item[3]), F32) for item in whole + square + joined],
         scratch_shapes=plain_scratch(items, kinds) + item_blocks(items, kinds, (), 2) + grp_scratch(items, kinds)
-        + grp_scratch(whole, whole_kinds) + grp_scratch(joined, joined_kinds),
+        + grp_scratch(whole, whole_kinds) + item_blocks(square, square_kinds, (), 2)
+        + quad_scratch(square, square_kinds) + grp_scratch(square, square_kinds) + grp_scratch(joined, joined_kinds),
         compiler_params=pltpu.CompilerParams(
             collective_id=collective_id, has_side_effects=True, vmem_limit_bytes=56 * MIB
         ),
         name="reduce_grads",
-    )(*sources, *held, *done)
+    )(*sources, *held, *quads, *done)
 
 
 def write_kernel(count, *refs):
@@ -1729,7 +1812,7 @@
      load_sem, store_sem, send_a, recv_a, local_a, send_b, recv_b, local_b) = rest[:35]
     me, peers = all_peers()
     reducer, near_devices = tok_steps(items, sources, rest[35:])
-    core_sends, core_sums, near_sums, first_sums, second_sums, finish = reducer
+    core_sends, core_sums, near_sums, first_sums, second_sums, finish = reducer[:6]
     odd, level_near, level_far = levels()
 
     def hold(item):
@@ -1802,10 +1885,6 @@
             near_sums(0)
             core_sums(1)
             core_sums(2)
-        else:
-            first_sums(0)
-            near_sums(1)
-            near_sums(2)
     loads["up"].wait()
     loads["mmid"].wait()
     loads["proj"].wait()
@@ -1848,10 +1927,13 @@
         )
 
     rows_back(0)
+    first_sums(0)
+    near_sums(1)
+    near_sums(2)
+    rows_back(1)
     hold(0)
     first_sums(1)
     first_sums(2)
-    rows_back(1)
     store(lup, lup_ref)
     store(agrad, agrad_ref)
     dmgain_ref[...] = mixer_gains[0] + mixer_gains[1]
@@ -1956,11 +2038,11 @@
         *scenes, keys, values, queries, attended_grad, figures, latents, upstream, query_gain[None], query_weight,
         d_first_gain, d_mixer_gain, d_second_gain,
     )
-    early, held = rest[:len(early)], rest[len(early):]
+    early, held, quads = rest[:len(early)], rest[len(early):len(early) + 1], rest[len(early) + 1:]
     o_output, o_key, o_value, o_query, gains, *late = reduce_grads(
-        7, [d_output, d_key, d_value, d_query, gains], held, early
+        7, [d_output, d_key, d_value, d_query, gains], held, quads, (False, True), early
     )
-    late, early = late[:len(held)], late[len(held):]
+    late, early = late[:3], late[3:]
     (latents_out, latents_grad, tokens_grad, o_second_up, o_second_down, o_mixer_output, o_first_up, o_first_down,
      o_project, o_output, o_key, o_value, o_query, *o_gains) = write_results(
         [latents_out, latents_grad.reshape(latents_out.shape), tokens_grad, *early, *late, o_output, o_key, o_value, o_query], gains, 5

time: 280 us -> 270 us (0.964)
  Pallas kernels: 275 us -> 265 us
    pallas_call x1, Pallas kernels: 66.9 us -> 60.3 us  [cross_backward(): pl.pallas_call(functools.partial(cross_backward_kernel, items, grad_items...]
    pallas_call x1, Pallas kernels: 61.2 us -> 57.9 us  [latents_backward(): pl.pallas_call(functools.partial(latents_backward_kernel, items), in_spec...]
where the time goes in v2:
time: 270 us; the launch traced here: 267 us
  Pallas kernels  265 us (98%)
    pallas_call x1, Pallas kernels, cross_backward(): pl.pallas_call(functools.partial(cross_backward_kernel, items, grad_items...  60.3 us
    pallas_call x1, Pallas kernels, latents_backward(): pl.pallas_call(functools.partial(latents_backward_kernel, items), in_spec...  57.9 us
    pallas_call x1, Pallas kernels, latents_forward(): pl.pallas_call(latents_forward_kernel, in_specs=[hbm, hbm, hbm, hbm, vmem...  54.2 us
    pallas_call x1, Pallas kernels, reduce_grads(): pl.pallas_call(functools.partial(reduce_kernel, items, whole, square, joi...  42.9 us
    pallas_call x1, Pallas kernels, cross_forward(): pl.pallas_call(cross_forward_kernel, in_specs=[hbm, hbm] + [vmem] * 5 + [...  41.2 us
    pallas_call x1, Pallas kernels, write_results(): pl.pallas_call(functools.partial(write_kernel, n), in_specs=[hbm] * n + [...  8.03 us

profile of v2, /device:TPU:0, one launch (start us, length us, event | category | flops | bytes accessed | tf_op | source)
XLA Modules:
  0.0 266.7 jit_solution(4879646811824461215)
XLA Ops:
  0.7 1.3 copy.39.count_ref
  2.0 41.2 %cross_forward.1 = (bf16[2,1024,512]{2,1,0:T(8,128)(2,1)}, bf16[2,1024,512]{2,1,0:T(8,128)(2,1)}, bf16[2,2048,512]{2,1,0:T(8,128)(2,1)}, f32[2,256,512]{2,1,0:T(8,128)}, f32[2,8,256]{2,1,0:T(8,128)}) custom-call(bf16[1,2,1024,512]{3,2,1,0:T(8,128)(2,1)} %tok_ref.3, f32[1,2,2048,512]{3,2,1,0:T(8,128)} %lat_ref.5, f32[1,512]{1,0:T(1,128)} %bitcast.33, ...), custom_call_target="tpu_custom_call" | custom-call | flops 14000000000 | bytes 22000000 | tf_op jit(solution)/shard_map/cross_forward/pallas_call | solution.py:667
  43.2 54.2 %latents_forward.1 = (f32[1,2,256,512]{3,2,1,0:T(8,128)}, f32[512,512]{1,0:T(8,128)}, f32[512,512]{1,0:T(8,128)}, bf16[3,2,64,2048]{3,2,1,0:T(8,128)(2,1)}, f32[...) custom-call(f32[1,2,2048,512]{3,2,1,0:T(8,128)} %lat_ref.5, ...), custom_call_target="tpu_custom_call" | custom-call | flops 20000000000 | bytes 30000000 | tf_op jit(solution)/shard_map/latents_forward/pallas_call | solution.py:1344
  97.4 57.9 %latents_backward.1 = (bf16[2,256,512]{2,1,0:T(8,128)(2,1)}, f32[2,8,256]{2,1,0:T(8,128)}, f32[512,512]{1,0:T(8,128)}, bf16[512,2048]{1,0:T(8,128)(2,1)}, bf16[2...) custom-call(bf16[1,8,64,512]{3,2,1,0:T(8,128)(2,1)} %get-tuple-eleme, ...), custom_call_target="tpu_custom_call" | custom-call | flops 35000000512 | bytes 36000000 | tf_op jit(solution)/shard_map/latents_backward/pallas_call | solution.py:1971
  155.3 60.3 %cross_backward.1 = (f32[512,512]{1,0:T(8,128)}, f32[1,2,1024,512]{3,2,1,0:T(8,128)}, bf16[512,512]{1,0:T(8,128)(2,1)}, bf16[512,512]{1,0:T(8,128)(2,1)}, bf16[5...) custom-call(bf16[1,2,1024,512]{3,2,1,0:T(8,128)(2,1)} %tok_ref.3, ...), custom_call_target="tpu_custom_call" | custom-call | flops 25999998976 | bytes 24000000 | tf_op jit(solution)/shard_map/cross_backward/pallas_call | solution.py:1125
  215.6 42.9 %reduce_grads.1 = (f32[64,512]{1,0:T(8,128)}, f32[64,512]{1,0:T(8,128)}, f32[64,512]{1,0:T(8,128)}, f32[64,512]{1,0:T(8,128)}, f32[16,128]{1,0:T(8,128)}, /*inde...) custom-call(bf16[2,2,2,64,512]{4,3,2,1,0:T(8,128)(2,1)} %bitcast.23,, ...), custom_call_target="tpu_custom_call" | custom-call | tf_op jit(solution)/shard_map/reduce_grads/pallas_call | solution.py:1752
  258.5 8.0 %write_results.1 = (f32[1,2,256,512]{3,2,1,0:T(8,128)}, f32[1,2,256,512]{3,2,1,0:T(8,128)}, f32[1,2,1024,512]{3,2,1,0:T(8,128)}, f32[64,2048]{1,0:T(8,128)}, f32...) custom-call(f32[1,2,256,512]{3,2,1,0:T(8,128)} %get-tuple-element.89, ...), custom_call_target="tpu_custom_call" | custom-call | tf_op jit(solution)/shard_map/write_results/pallas_call | solution.py:1788

commit v3 on v2

--- a/solution.py
+++ b/solution.py
@@ -472,7 +472,7 @@
     for member in range(MB):
         scene = lax.broadcasted_iota(jnp.int32, (SCENES, TOK_DEV), 0)
         place = lax.broadcasted_iota(jnp.int32, (SCENES, TOK_DEV), 1)
-        hot = jnp.where((seg_buf[member:member + 1] == scene) & (place < count_ref[0, member, 0]), 1.0, 0.0)
+        hot = jnp.where((seg_buf[member:member + 1] == scene) & (place < count_ref[member]), 1.0, 0.0)
         seen = tn(jnp.where(mask_buf[member] > 0, 1.0, 0.0).astype(BF16), hot.astype(BF16))
         bias_ref[member] = jnp.where(seen > 0.5, 0.0, NEG)
 
@@ -2019,7 +2019,7 @@
     second_down,
     cotangent,
 ):
-    scenes = (segments, scene_mask, counts)
+    scenes = (segments, scene_mask, counts.reshape(MB))
     keys, values, queries, attended, lse = cross_forward(
         0, tokens, latents, token_gain[None], query_gain[None], query_weight, key_weight, value_weight, *scenes
     )

time: 270 us -> 269 us (level)
  no operation moved by 1% of the time
where the time goes in v3:
time: 269 us; the launch traced here: 265 us
  Pallas kernels  264 us (98%)
    pallas_call x1, Pallas kernels, cross_backward(): pl.pallas_call(functools.partial(cross_backward_kernel, items, grad_items...  60.2 us
    pallas_call x1, Pallas kernels, latents_backward(): pl.pallas_call(functools.partial(latents_backward_kernel, items), in_spec...  57.9 us
    pallas_call x1, Pallas kernels, latents_forward(): pl.pallas_call(latents_forward_kernel, in_specs=[hbm, hbm, hbm, hbm, vmem...  54.2 us
    pallas_call x1, Pallas kernels, reduce_grads(): pl.pallas_call(functools.partial(reduce_kernel, items, whole, square, joi...  42.8 us
    pallas_call x1, Pallas kernels, cross_forward(): pl.pallas_call(cross_forward_kernel, in_specs=[hbm, hbm] + [vmem] * 5 + [...  41.2 us
    pallas_call x1, Pallas kernels, write_results(): pl.pallas_call(functools.partial(write_kernel, n), in_specs=[hbm] * n + [...  8.03 us

profile of v3, /device:TPU:0, one launch (start us, length us, event | category | flops | bytes accessed | tf_op | source)
XLA Modules:
  0.0 265.3 jit_solution(3244254370420917180)
XLA Ops:
  0.7 41.2 %cross_forward.1 = (bf16[2,1024,512]{2,1,0:T(8,128)(2,1)}, bf16[2,1024,512]{2,1,0:T(8,128)(2,1)}, bf16[2,2048,512]{2,1,0:T(8,128)(2,1)}, f32[2,256,512]{2,1,0:T(8,128)}, f32[2,8,256]{2,1,0:T(8,128)}) custom-call(bf16[1,2,1024,512]{3,2,1,0:T(8,128)(2,1)} %tok_ref.3, f32[1,2,2048,512]{3,2,1,0:T(8,128)} %lat_ref.5, f32[1,512]{1,0:T(1,128)} %bitcast.34, ...), custom_call_target="tpu_custom_call" | custom-call | flops 14000000000 | bytes 22000000 | tf_op jit(solution)/shard_map/cross_forward/pallas_call | solution.py:667
  41.9 54.2 %latents_forward.1 = (f32[1,2,256,512]{3,2,1,0:T(8,128)}, f32[512,512]{1,0:T(8,128)}, f32[512,512]{1,0:T(8,128)}, bf16[3,2,64,2048]{3,2,1,0:T(8,128)(2,1)}, f32[...) custom-call(f32[1,2,2048,512]{3,2,1,0:T(8,128)} %lat_ref.5, ...), custom_call_target="tpu_custom_call" | custom-call | flops 20000000000 | bytes 30000000 | tf_op jit(solution)/shard_map/latents_forward/pallas_call | solution.py:1344
  96.1 57.9 %latents_backward.1 = (bf16[2,256,512]{2,1,0:T(8,128)(2,1)}, f32[2,8,256]{2,1,0:T(8,128)}, f32[512,512]{1,0:T(8,128)}, bf16[512,2048]{1,0:T(8,128)(2,1)}, bf16[2...) custom-call(bf16[1,8,64,512]{3,2,1,0:T(8,128)(2,1)} %get-tuple-eleme, ...), custom_call_target="tpu_custom_call" | custom-call | flops 35000000512 | bytes 36000000 | tf_op jit(solution)/shard_map/latents_backward/pallas_call | solution.py:1971
  154.0 60.2 %cross_backward.1 = (f32[512,512]{1,0:T(8,128)}, f32[1,2,1024,512]{3,2,1,0:T(8,128)}, bf16[512,512]{1,0:T(8,128)(2,1)}, bf16[512,512]{1,0:T(8,128)(2,1)}, bf16[5...) custom-call(bf16[1,2,1024,512]{3,2,1,0:T(8,128)(2,1)} %tok_ref.3, ...), custom_call_target="tpu_custom_call" | custom-call | flops 25999998976 | bytes 24000000 | tf_op jit(solution)/shard_map/cross_backward/pallas_call | solution.py:1125
  214.3 42.8 %reduce_grads.1 = (f32[64,512]{1,0:T(8,128)}, f32[64,512]{1,0:T(8,128)}, f32[64,512]{1,0:T(8,128)}, f32[64,512]{1,0:T(8,128)}, f32[16,128]{1,0:T(8,128)}, /*inde...) custom-call(bf16[2,2,2,64,512]{4,3,2,1,0:T(8,128)(2,1)} %bitcast.24,, ...), custom_call_target="tpu_custom_call" | custom-call | tf_op jit(solution)/shard_map/reduce_grads/pallas_call | solution.py:1752
  257.1 8.0 %write_results.1 = (f32[1,2,256,512]{3,2,1,0:T(8,128)}, f32[1,2,256,512]{3,2,1,0:T(8,128)}, f32[1,2,1024,512]{3,2,1,0:T(8,128)}, f32[64,2048]{1,0:T(8,128)}, f32...) custom-call(f32[1,2,256,512]{3,2,1,0:T(8,128)} %get-tuple-element.89, ...), custom_call_target="tpu_custom_call" | custom-call | tf_op jit(solution)/shard_map/write_results/pallas_call | solution.py:1788

commit v4 on v3

--- a/solution.py
+++ b/solution.py
@@ -1759,23 +1759,24 @@
         + grp_scratch(whole, whole_kinds) + item_blocks(square, square_kinds, (), 2)
         + quad_scratch(square, square_kinds) + grp_scratch(square, square_kinds) + grp_scratch(joined, joined_kinds),
         compiler_params=pltpu.CompilerParams(
-            collective_id=collective_id, has_side_effects=True, vmem_limit_bytes=56 * MIB
+            collective_id=collective_id, has_side_effects=True, vmem_limit_bytes=48 * MIB
         ),
         name="reduce_grads",
     )(*sources, *held, *quads, *done)
 
 
-def write_kernel(count, *refs):
+def write_kernel(count, large, *refs):
     sources, gain_ref, outs = refs[:count], refs[count], refs[count + 1:2 * count + 1]
-    gain_outs, buffers = refs[2 * count + 1:-count - 2], refs[-count - 2:-2]
+    gain_outs, buffers = refs[2 * count + 1:-large - 2], refs[-large - 2:-2]
     in_sem, out_sem = refs[-2:]
-    ins = [pltpu.make_async_copy(sources[i], buffers[i], in_sem.at[i]) for i in range(count)]
-    backs = [pltpu.make_async_copy(buffers[i], outs[i], out_sem.at[i]) for i in range(count)]
-    for copy in ins:
+    ins = [pltpu.make_async_copy(sources[i], buffers[i], in_sem.at[i]) for i in range(large)]
+    held = buffers + sources[large:]
+    backs = [pltpu.make_async_copy(held[i], outs[i], out_sem.at[i]) for i in range(count)]
+    for copy in ins + backs[large:]:
         copy.start()
     for i, out in enumerate(gain_outs):
         out[...] = gain_ref[i:i + 1, 0:D // TOK]
-    for i in range(count):
+    for i in range(large):
         ins[i].wait()
         backs[i].start()
     for copy in backs:
@@ -1784,16 +1785,17 @@
 
 def write_results(results, gains, gain_count):
     n = len(results)
+    large = sum(result.ndim == 4 for result in results)
     hbm, vmem = pl.BlockSpec(memory_space=pl.ANY), pl.BlockSpec(memory_space=pltpu.VMEM)
     return pl.pallas_call(
-        functools.partial(write_kernel, n),
-        in_specs=[hbm] * n + [vmem],
+        functools.partial(write_kernel, n, large),
+        in_specs=[hbm] * large + [vmem] * (n - large + 1),
         out_specs=[hbm] * n + [vmem] * gain_count,
         out_shape=[jax.ShapeDtypeStruct(result.shape, result.dtype) for result in results]
         + [jax.ShapeDtypeStruct((1, D // TOK), F32)] * gain_count,
-        scratch_shapes=[pltpu.VMEM(result.shape, result.dtype) for result in results]
-        + [pltpu.SemaphoreType.DMA((n,)), pltpu.SemaphoreType.DMA((n,))],
-        compiler_params=pltpu.CompilerParams(vmem_limit_bytes=60 * MIB),
+        scratch_shapes=[pltpu.VMEM(result.shape, result.dtype) for result in results[:large]]
+        + [pltpu.SemaphoreType.DMA((large,)), pltpu.SemaphoreType.DMA((n,))],
+        compiler_params=pltpu.CompilerParams(vmem_limit_bytes=56 * MIB),
         name="write_results",
     )(*results, gains)
 

time: 269 us -> 285 us (1.059)
  local copies, waits for them, and re-layouts: 0 us -> 16.3 us
    unnamed x0 -> x42, local copies, waits for them, and re-layouts: none -> 16.3 us
where the time goes in v4:
time: 285 us; the launch traced here: 281 us
  Pallas kernels  264 us (93%)
  local copies, waits for them, and re-layouts  16.3 us (6%)
    pallas_call x1, Pallas kernels, cross_backward(): pl.pallas_call(functools.partial(cross_backward_kernel, items, grad_items...  60.2 us
    pallas_call x1, Pallas kernels, latents_backward(): pl.pallas_call(functools.partial(latents_backward_kernel, items), in_spec...  57.9 us
    pallas_call x1, Pallas kernels, latents_forward(): pl.pallas_call(latents_forward_kernel, in_specs=[hbm, hbm, hbm, hbm, vmem...  54.2 us
    pallas_call x1, Pallas kernels, reduce_grads(): pl.pallas_call(functools.partial(reduce_kernel, items, whole, square, joi...  41.2 us
    pallas_call x1, Pallas kernels, cross_forward(): pl.pallas_call(cross_forward_kernel, in_specs=[hbm, hbm] + [vmem] * 5 + [...  41.2 us
    unnamed x42, local copies, waits for them, and re-layouts  16.3 us
    pallas_call x1, Pallas kernels, write_results(): pl.pallas_call(functools.partial(write_kernel, n, large), in_specs=[hbm]...  9.22 us

profile of v4, /device:TPU:0, one launch (start us, length us, event | category | flops | bytes accessed | tf_op | source)
XLA Modules:
  0.0 281.2 jit_solution(17977833633534303117)
XLA Ops:
  0.7 41.2 %cross_forward.1 = (bf16[2,1024,512]{2,1,0:T(8,128)(2,1)}, bf16[2,1024,512]{2,1,0:T(8,128)(2,1)}, bf16[2,2048,512]{2,1,0:T(8,128)(2,1)}, f32[2,256,512]{2,1,0:T(8,128)}, f32[2,8,256]{2,1,0:T(8,128)}) custom-call(bf16[1,2,1024,512]{3,2,1,0:T(8,128)(2,1)} %tok_ref.3, f32[1,2,2048,512]{3,2,1,0:T(8,128)} %lat_ref.5, f32[1,512]{1,0:T(1,128)} %bitcast.34, ...), custom_call_target="tpu_custom_call" | custom-call | flops 14000000000 | bytes 22000000 | tf_op jit(solution)/shard_map/cross_forward/pallas_call | solution.py:667
  41.9 54.2 %latents_forward.1 = (f32[1,2,256,512]{3,2,1,0:T(8,128)}, f32[512,512]{1,0:T(8,128)}, f32[512,512]{1,0:T(8,128)}, bf16[3,2,64,2048]{3,2,1,0:T(8,128)(2,1)}, f32[...) custom-call(f32[1,2,2048,512]{3,2,1,0:T(8,128)} %lat_ref.5, ...), custom_call_target="tpu_custom_call" | custom-call | flops 20000000000 | bytes 30000000 | tf_op jit(solution)/shard_map/latents_forward/pallas_call | solution.py:1344
  96.1 57.9 %latents_backward.1 = (bf16[2,256,512]{2,1,0:T(8,128)(2,1)}, f32[2,8,256]{2,1,0:T(8,128)}, f32[512,512]{1,0:T(8,128)}, bf16[512,2048]{1,0:T(8,128)(2,1)}, bf16[2...) custom-call(bf16[1,8,64,512]{3,2,1,0:T(8,128)(2,1)} %get-tuple-eleme, ...), custom_call_target="tpu_custom_call" | custom-call | flops 35000000512 | bytes 36000000 | tf_op jit(solution)/shard_map/latents_backward/pallas_call | solution.py:1973
  154.0 0.0 copy-start
  154.0 60.2 %cross_backward.1 = (f32[512,512]{1,0:T(8,128)}, f32[1,2,1024,512]{3,2,1,0:T(8,128)}, bf16[512,512]{1,0:T(8,128)(2,1)}, bf16[512,512]{1,0:T(8,128)(2,1)}, bf16[5...) custom-call(bf16[1,2,1024,512]{3,2,1,0:T(8,128)(2,1)} %tok_ref.3, ...), custom_call_target="tpu_custom_call" | custom-call | flops 25999998976 | bytes 24000000 | tf_op jit(solution)/shard_map/cross_backward/pallas_call | solution.py:1125
  214.3 0.0 copy-done
  214.3 0.0 copy-start.1
  214.3 1.0 copy-done.1
  215.3 0.0 copy-start.2
  215.3 1.0 copy-done.2
  216.4 0.0 copy-start.3
  216.4 1.0 copy-done.3
  217.4 0.0 copy-start.8
  217.4 1.0 copy-done.8
  218.4 0.0 copy-start.15
  218.4 0.9 copy-done.15
  219.3 0.0 copy-start.16
  219.3 0.9 copy-done.16
  220.2 0.0 copy-start.17
  220.2 0.9 copy-done.17
  221.1 0.0 copy-start.18
  221.1 0.8 copy-done.18
  222.0 0.0 copy-start.19
  222.0 0.8 copy-done.19
  222.7 41.2 %reduce_grads.1 = (f32[64,512]{1,0:T(8,128)S(1)}, f32[64,512]{1,0:T(8,128)S(1)}, f32[64,512]{1,0:T(8,128)S(1)}, f32[64,512]{1,0:T(8,128)S(1)}, f32[16,128]{1,0:T...) custom-call(bf16[2,2,2,64,512]{4,3,2,1,0:T(8,128)(2,1)S(1)} %bitcast, ...), custom_call_target="tpu_custom_call" | custom-call | tf_op jit(solution)/shard_map/reduce_grads/pallas_call | solution.py:1752
  263.9 0.0 copy-start.4
  263.9 0.8 copy-done.4
  264.7 0.0 copy-start.5
  264.7 0.8 copy-done.5
  265.6 0.0 copy-start.6
  265.6 0.8 copy-done.6
  266.4 0.0 copy-start.7
  266.4 0.8 copy-done.7
  267.1 0.0 copy-start.9
  267.2 0.8 copy-done.9
  267.9 0.0 copy-start.10
  267.9 0.6 copy-done.10
  268.6 0.0 copy-start.11
  268.6 0.7 copy-done.11
  269.2 0.0 copy-start.12
  269.2 0.7 copy-done.12
  269.9 0.0 copy-start.13
  269.9 0.6 copy-done.13
  270.5 0.0 copy-start.14
  270.5 0.7 copy-done.14
  271.2 0.0 copy-start.20
  271.2 0.6 copy-done.20
  271.8 9.2 %write_results.1 = (f32[1,2,256,512]{3,2,1,0:T(8,128)}, f32[1,2,256,512]{3,2,1,0:T(8,128)}, f32[1,2,1024,512]{3,2,1,0:T(8,128)}, f32[64,2048]{1,0:T(8,128)}, f32...) custom-call(f32[1,2,256,512]{3,2,1,0:T(8,128)} %get-tuple-element.89, ...), custom_call_target="tpu_custom_call" | custom-call | tf_op jit(solution)/shard_map/write_results/pallas_call | solution.py:1790
Async XLA Ops:
  154.0 60.2 %copy-start = (bf16[512,512]{1,0:T(8,128)(2,1)S(1)}, bf16[512,512]{1,0:T(8,128)(2,1)}, u32[]{:S(2)}) copy-start(bf16[512,512]{1,0:T(8,128)(2,1)} %get-tuple-element.118) | copy-start | bytes 1572868
  214.3 1.0 copy-start.1
  215.3 1.0 copy-start.2
  216.4 1.0 copy-start.3
  217.4 1.0 copy-start.8
  218.4 0.9 copy-start.15
  219.3 0.9 copy-start.16
  220.2 0.9 copy-start.17
  221.1 0.8 copy-start.18
  222.0 0.8 copy-start.19
  263.9 0.8 copy-start.4
  264.7 0.8 copy-start.5
  265.6 0.8 copy-start.6
  266.4 0.8 copy-start.7
  267.1 0.8 copy-start.9
  267.9 0.7 copy-start.10
  268.6 0.7 copy-start.11
  269.2 0.7 copy-start.12
  269.9 0.6 copy-start.13
  270.5 0.7 copy-start.14
  271.2 0.6 copy-start.20
